TPU v7x, 1024 devices: a whole 4x8x16 slice. The times are simulated.
1024 devices in a mesh: gx: 8 (over z_lo, core), gy: 4 (over x), gz: 32 (over z_hi, y).
Axes of the slice: x: 4, y: 8, z: 16 (z_hi: 4, z_lo: 4; z = z_hi * 4 + z_lo), core: 2. Of those that a mesh axis runs over, the one named last changes fastest.
Arguments:
- rhs: float32 [32, 16, 1024, 512], P('gx', 'gy', 'gz'), may hold values from -6 to 6
- coef: float32 [32, 16, 1024], P('gx', 'gy', 'gz'), may hold values from 1 to 4
- mass: float32 [512, 512], replicated, as said below
- smoother: float32 [512, 512], replicated, as said below
- lift: float32 [384, 512], replicated, may hold values from -0.15 to 0.15
- restrict: float32 [512, 8], replicated, may hold values from -0.25 to 0.25
- coarse_block_matrix: float32 [8, 8], replicated
- element_cluster_index: int32 [32, 16, 1024], P('gx', 'gy', 'gz'), may hold values from 0 to 63
Outputs:
- corrected: float32 [32, 16, 1024, 512], P('gx', 'gy', 'gz')
Inputs may be any that keep to these rules, and one draw needn't show every extreme that they name: `element_cluster_index`: index of an agglomerate within the element's own device block. `mass`: identity plus independent entries of deviation 0.15 / sqrt(512). `smoother`: identity minus the off-diagonal part of mass.
All inputs are finite; a program needn't handle non-finite values.
Results may differ from a plain program's by a relative error of at most 0.00005.
Values sent between devices are 32-bit elements; how exact they have to be, the bound alone decides.
A program may use at most 64 MiB of HBM per device.

v0:
```python
import jax
import jax.numpy as jnp
from jax import lax
from jax.sharding import PartitionSpec as P

EDGE = 8
ELEMENT_DOFS = 512
FACE = 64
COARSE = 8
DEVICE_CLUSTERS = 64


def extended(cells, sides, width):
    for axis, dim in sides:
        count = lax.axis_size(axis)
        ends = count - 1
        head = lax.slice_in_dim(cells, 0, width, axis=dim)
        tail = lax.slice_in_dim(cells, cells.shape[dim] - width, cells.shape[dim], axis=dim)
        cells = jnp.concatenate(
            [
                lax.ppermute(tail, axis, [(i, (i + 1) % count) for i in range(ends)]),
                cells,
                lax.ppermute(head, axis, [((i + 1) % count, i) for i in range(ends)]),
            ],
            axis=dim,
        )
    return cells


def face_traces(field):
    cube = field.reshape(field.shape[:-1] + (EDGE, EDGE, EDGE))
    lead = field.shape[:-1]
    last = EDGE - 1
    parts = [
        cube[..., 0, :, :],
        cube[..., last, :, :],
        cube[..., :, 0, :],
        cube[..., :, last, :],
        cube[..., :, :, 0],
        cube[..., :, :, last],
    ]
    return jnp.concatenate([p.reshape(lead + (FACE,)) for p in parts], -1)


def neighbour_faces(padded):
    width = FACE
    return jnp.concatenate(
        [
            padded[:-2, 1:-1, 1:-1, width : 2 * width],
            padded[2:, 1:-1, 1:-1, 0:width],
            padded[1:-1, :-2, 1:-1, 3 * width : 4 * width],
            padded[1:-1, 2:, 1:-1, 2 * width : 3 * width],
            padded[1:-1, 1:-1, :-2, 5 * width : 6 * width],
            padded[1:-1, 1:-1, 2:, 4 * width : 5 * width],
        ],
        -1,
    )


def shards(rhs, coef, mass, smoother, lift, restrict, coarse_block_matrix, element_cluster_index):
    high = lax.Precision.HIGHEST

    def mult(a, b):
        return jnp.matmul(a, b, precision=high)

    def operate(field):
        padded = extended(face_traces(field), (("gx", 0), ("gy", 1), ("gz", 2)), 1)
        faces = neighbour_faces(padded)
        return coef[..., None] * mult(field, mass) - mult(faces, lift)

    first = mult(rhs, smoother) / coef[..., None]
    second = first + mult(rhs - operate(first), smoother) / coef[..., None]
    resid = rhs - operate(second)
    small = mult(resid.reshape(-1, ELEMENT_DOFS), restrict)
    labels = element_cluster_index.reshape(-1)
    onehot = (labels[:, None] == jnp.arange(DEVICE_CLUSTERS, dtype=jnp.int32)[None, :]).astype(
        jnp.float32
    )
    local_rhs = mult(small.T, onehot)
    counts = jnp.sum(onehot, 0)[None, :]
    coarse_rhs, column_counts = (
        lax.all_gather(local_rhs, "gx", axis=1, tiled=True),
        lax.all_gather(counts, "gx", axis=1, tiled=True),
    )
    weight_factor = 1.0 + column_counts
    zone = coarse_rhs / weight_factor
    zpad = extended(zone[None, None], (("gy", 0), ("gz", 1)), 1)
    nearby = zpad[0, 1] + zpad[2, 1] + zpad[1, 0] + zpad[1, 2]
    blocks_along = zone.shape[1] // DEVICE_CLUSTERS
    line_sum = jnp.sum(zone.reshape(COARSE, blocks_along, DEVICE_CLUSTERS), 1, keepdims=True)
    line_sum = jnp.broadcast_to(line_sum, (COARSE, blocks_along, DEVICE_CLUSTERS)).reshape(
        zone.shape
    )
    applied = weight_factor * mult(coarse_block_matrix, zone) - nearby - line_sum
    ztwo = zone + (coarse_rhs - applied) / weight_factor
    mine = lax.dynamic_slice_in_dim(
        ztwo, lax.axis_index("gx") * DEVICE_CLUSTERS, DEVICE_CLUSTERS, 1
    )
    corr = mult(mult(onehot, mine.T), restrict.T)
    return second + corr.reshape(second.shape)


def solution(mesh):
    return jax.shard_map(
        shards,
        mesh=mesh,
        in_specs=(
            P("gx", "gy", "gz", None),
            P("gx", "gy", "gz"),
            P(),
            P(),
            P(),
            P(),
            P(),
            P("gx", "gy", "gz"),
        ),
        out_specs=P("gx", "gy", "gz", None),
        check_vma=False,
    )
```

profile of v0, /device:TPU:58, one launch (start us, length us, event | category | flops | bytes accessed | tf_op | source)
XLA Modules:
  0.0 203.9 jit_solution(13616990778783640945)
XLA Ops:
  1.2 3.1 %convolution_divide_fusion.1 = f32[4,4,32,512]{3,2,1,0:T(8,128)S(1)} fusion(f32[4,4,32,512]{3,2,1,0:T(8,128)} %param.8, f32[512,512]{1,0:T(8,128)S(1)} %copy-done, f32[4,4,32]{2,1,0:T(4,128)} %param.9), kind=kOutput, calls=%fused_computation.7 | convolution fusion | flops 1610874880 | bytes 3147776 | tf_op jit(solution)/shard_map/dot_general | solution.py:64
  4.3 2.7 %copy.33 = f32[4,4,32,512]{2,3,1,0:T(8,128)} copy(f32[4,4,32,512]{3,2,1,0:T(8,128)S(1)} %convolution_divide_fusion.1) | data formatting | bytes 2097152 | tf_op jit(solution)/shard_map/div | solution.py:71
  7.0 2.1 %slice_bitcast_fusion.6 = (f32[4,4,32,64]{2,3,1,0:T(8,128)S(1)}, f32[4,4,32,64]{2,3,1,0:T(8,128)}) fusion(f32[4,4,32,8,8,8]{2,5,4,3,1,0:T(8,128)} %bitcast.77), kind=kLoop, calls=%fused_computation.25 | loop fusion | bytes 524288 | tf_op jit(solution)/shard_map/reshape;squeeze | solution.py:42
  9.1 2.3 %slice_bitcast_fusion.4 = (f32[4,4,32,64]{2,3,1,0:T(8,128)}, f32[4,4,32,64]{2,3,1,0:T(8,128)}) fusion(f32[4,4,32,8,8,8]{2,5,4,3,1,0:T(8,128)} %bitcast.78), kind=kLoop, calls=%fused_computation.23 | loop fusion | bytes 524288 | tf_op jit(solution)/shard_map/reshape;squeeze | solution.py:42
  11.5 5.4 %fusion.21 = (f32[4,4,32,8,8,1]{2,5,4,3,1,0:T(1,128)S(1)}, f32[4,4,32,8,8,1]{2,5,4,3,1,0:T(1,128)}) fusion(f32[4,4,32,8,8,8]{2,5,4,3,1,0:T(8,128)} %bitcast.79), kind=kLoop, calls=%fused_computation.99 | loop fusion | bytes 524288 | tf_op jit(solution)/shard_map/slice | solution.py:40
  16.9 1.9 copy.34
  19.8 2.0 %copy.36 = f32[4,4,32,64]{3,2,1,0:T(8,128)} copy(f32[4,4,32,64]{2,3,1,0:T(8,128)} %get-tuple-element.14) | data formatting | bytes 262144 | tf_op jit(solution)/shard_map/reshape;squeeze | solution.py:42
  21.8 1.9 copy.37
  23.8 1.9 copy.38
  26.6 1.7 concatenate.65
  29.0 1.7 collective-permute-start
  32.1 1.3 dynamic-slice
  34.4 20.5 %all-reduce = f32[512]{0:T(512)S(1)} all-reduce(f32[512]{0:T(512)S(1)} %dynamic-update-slice), channel_id=2, replica_groups=mesh['gx'=8,'gy'=4,'gz'=32] {'gx'}, use_global_device_ids=true, to_apply=%add | all-reduce | flops 512 | bytes 4096
  54.9 2.4 %collective-permute-start.3 = (f32[6,1,32,384]{3,2,1,0:T(8,128)S(1)}, f32[6,1,32,384]{3,2,1,0:T(8,128)S(1)}, u32[]{:S(2)}, u32[]{:S(2)}) collective-permute-start(f32[6,1,32,384]{3,2,1,0:T(8,128)S(1)} %get-tuple-element.29), channel_id=1, source_target_pairs={{32,0},{64,32},{96,64},{33,1},{65,33},{97,65},{34,2},{66,34},{98,6... | collective-permute-start | bytes 884744 | tf_op jit(solution)/shard_map/ppermute | solution.py:23
  57.4 3.4 %collective-permute-start.2 = (f32[6,1,32,384]{3,2,1,0:T(8,128)S(1)}, f32[6,1,32,384]{3,2,1,0:T(8,128)S(1)}, u32[]{:S(2)}, u32[]{:S(2)}) collective-permute-start(f32[6,1,32,384]{3,2,1,0:T(8,128)S(1)} %get-tuple-element.30), channel_id=1, source_target_pairs={{0,32},{32,64},{64,96},{1,33},{33,65},{65,97},{2,34},{34,66},{66,9... | collective-permute-start | bytes 884744 | tf_op jit(solution)/shard_map/ppermute | solution.py:21
  60.8 4.1 %convolution_multiply_fusion.1 = f32[4,4,32,512]{3,2,1,0:T(8,128)} fusion(f32[4,4,32,512]{3,2,1,0:T(8,128)} %copy-done.2, f32[512,512]{1,0:T(8,128)S(1)} %copy-done.1, f32[4,4,32]{2,1,0:T(4,128)S(1)} %copy-done.5), kind=kOutput, calls=%fused_computation.6 | convolution fusion | flops 1610874880 | bytes 3147776 | tf_op jit(solution)/shard_map/dot_general | solution.py:64
  66.1 10.1 %collective-permute-start.4 = (f32[6,6,1,384]{3,2,1,0:T(1,128)S(1)}, f32[6,6,1,384]{3,2,1,0:T(1,128)S(1)}, u32[]{:S(2)}, u32[]{:S(2)}) collective-permute-start(f32[6,6,1,384]{3,2,1,0:T(1,128)S(1)} %get-tuple-element.24), channel_id=1, source_target_pairs={{0,1},{1,2},{2,3},{3,4},{4,5},{5,6},{6,7},{7,8},{8,9},{9,10},{10,1... | collective-permute-start | bytes 165896 | tf_op jit(solution)/shard_map/ppermute | solution.py:21
  76.2 2.1 %collective-permute-start.5 = (f32[6,6,1,384]{3,2,1,0:T(1,128)S(1)}, f32[6,6,1,384]{3,2,1,0:T(1,128)S(1)}, u32[]{:S(2)}, u32[]{:S(2)}) collective-permute-start(f32[6,6,1,384]{3,2,1,0:T(1,128)S(1)} %get-tuple-element.23), channel_id=1, source_target_pairs={{1,0},{2,1},{3,2},{4,3},{5,4},{6,5},{7,6},{8,7},{9,8},{10,9},{11,1... | collective-permute-start | bytes 165896 | tf_op jit(solution)/shard_map/ppermute | solution.py:23
  79.1 9.8 %collective-permute-done.5 = f32[6,6,1,384]{3,2,1,0:T(1,128)S(1)} collective-permute-done((f32[6,6,1,384]{3,2,1,0:T(1,128)S(1)}, f32[6,6,1,384]{3,2,1,0:T(1,128)S(1)}, u32[]{:S(2)}, u32[]{:S(2)}) %collective-permute-start.5) | collective-permute-done | bytes 55328 | tf_op jit(solution)/shard_map/ppermute | solution.py:23
  90.2 1.6 concatenate.74
  91.8 3.4 %fusion.2 = f32[4,4,32,512]{3,2,1,0:T(8,128)S(1)} fusion(f32[4,4,32,512]{3,2,1,0:T(8,128)} %param.8, f32[4,4,32,512]{3,2,1,0:T(8,128)S(1)} %copy-done.3, f32[4,4,32,384]{3,2,1,0:T(8,128)S(1)} %concatenate.74, f32[384,512]{1,0:T(8,128)} %param.12), kind=kOutput, calls=%fused_computation.8 | convolution fusion | flops 1208483840 | bytes 4718592 | tf_op jit(solution)/shard_map/dot_general | solution.py:64
  95.2 3.1 %fusion.1 = f32[4,4,32,512]{3,2,1,0:T(8,128)S(1)} fusion(f32[4,4,32,512]{3,2,1,0:T(8,128)} %copy-done.2, f32[4,4,32,512]{3,2,1,0:T(8,128)S(1)} %fusion.2, f32[512,512]{1,0:T(8,128)S(1)} %copy-done, f32[4,4,32]{2,1,0:T(4,128)S(1)} %copy-done.5), kind=kOutput, calls=%fused_computation.5 | convolution fusion | flops 1611137024 | bytes 4196352 | tf_op jit(solution)/shard_map/dot_general | solution.py:64
  98.3 2.7 %copy.40 = f32[4,4,32,512]{2,3,1,0:T(8,128)} copy(f32[4,4,32,512]{3,2,1,0:T(8,128)S(1)} %fusion.1) | data formatting | bytes 2097152 | tf_op jit(solution)/shard_map/add | solution.py:72
  100.9 2.3 %slice_bitcast_fusion.2 = (f32[4,4,32,64]{2,3,1,0:T(8,128)}, f32[4,4,32,64]{2,3,1,0:T(8,128)}) fusion(f32[4,4,32,8,8,8]{2,5,4,3,1,0:T(8,128)} %bitcast.80), kind=kLoop, calls=%fused_computation.21 | loop fusion | bytes 524288 | tf_op jit(solution)/shard_map/reshape;squeeze | solution.py:42
  103.2 2.3 %slice_bitcast_fusion = (f32[4,4,32,64]{2,3,1,0:T(8,128)}, f32[4,4,32,64]{2,3,1,0:T(8,128)}) fusion(f32[4,4,32,8,8,8]{2,5,4,3,1,0:T(8,128)} %bitcast.81), kind=kLoop, calls=%fused_computation.19 | loop fusion | bytes 524288 | tf_op jit(solution)/shard_map/reshape;squeeze | solution.py:42
  105.6 4.6 %fusion.20 = (f32[4,4,32,8,8,1]{2,5,4,3,1,0:T(1,128)S(1)}, f32[4,4,32,8,8,1]{2,5,4,3,1,0:T(1,128)S(1)}) fusion(f32[4,4,32,8,8,8]{2,5,4,3,1,0:T(8,128)} %bitcast.82), kind=kLoop, calls=%fused_computation.98 | loop fusion | bytes 524288 | tf_op jit(solution)/shard_map/slice | solution.py:40
  110.2 1.9 copy.41
  112.1 1.9 copy.42
  114.1 1.9 copy.43
  116.0 2.0 copy.44
  119.0 1.6 concatenate.75
  123.4 1.9 collective-permute-done.7
  125.4 2.0 %collective-permute-start.9 = (f32[6,1,32,384]{3,2,1,0:T(8,128)S(1)}, f32[6,1,32,384]{3,2,1,0:T(8,128)S(1)}, u32[]{:S(2)}, u32[]{:S(2)}) collective-permute-start(f32[6,1,32,384]{3,2,1,0:T(8,128)S(1)} %get-tuple-element.27), channel_id=1, source_target_pairs={{32,0},{64,32},{96,64},{33,1},{65,33},{97,65},{34,2},{66,34},{98,6... | collective-permute-start | bytes 884744 | tf_op jit(solution)/shard_map/ppermute | solution.py:23
  127.4 3.8 %collective-permute-start.8 = (f32[6,1,32,384]{3,2,1,0:T(8,128)S(1)}, f32[6,1,32,384]{3,2,1,0:T(8,128)S(1)}, u32[]{:S(2)}, u32[]{:S(2)}) collective-permute-start(f32[6,1,32,384]{3,2,1,0:T(8,128)S(1)} %get-tuple-element.28), channel_id=1, source_target_pairs={{0,32},{32,64},{64,96},{1,33},{33,65},{65,97},{2,34},{34,66},{66,9... | collective-permute-start | bytes 884744 | tf_op jit(solution)/shard_map/ppermute | solution.py:21
  131.3 4.0 %convolution_multiply_fusion = f32[4,4,32,512]{3,2,1,0:T(8,128)} fusion(f32[4,4,32,512]{3,2,1,0:T(8,128)S(1)} %fusion.1, f32[512,512]{1,0:T(8,128)} %param.10, f32[4,4,32]{2,1,0:T(4,128)S(1)} %copy-done.5), kind=kOutput, calls=%fused_computation.3 | convolution fusion | flops 1610874880 | bytes 3147776 | tf_op jit(solution)/shard_map/dot_general | solution.py:64
  135.8 2.2 %collective-permute-done.8 = f32[6,1,32,384]{3,2,1,0:T(8,128)S(1)} collective-permute-done((f32[6,1,32,384]{3,2,1,0:T(8,128)S(1)}, f32[6,1,32,384]{3,2,1,0:T(8,128)S(1)}, u32[]{:S(2)}, u32[]{:S(2)}) %collective-permute-start.8) | collective-permute-done | bytes 294944 | tf_op jit(solution)/shard_map/ppermute | solution.py:21
  138.1 2.0 collective-permute-start.10
  140.1 3.8 %collective-permute-start.11 = (f32[6,6,1,384]{3,2,1,0:T(1,128)S(1)}, f32[6,6,1,384]{3,2,1,0:T(1,128)S(1)}, u32[]{:S(2)}, u32[]{:S(2)}) collective-permute-start(f32[6,6,1,384]{3,2,1,0:T(1,128)S(1)} %get-tuple-element.19), channel_id=1, source_target_pairs={{1,0},{2,1},{3,2},{4,3},{5,4},{6,5},{7,6},{8,7},{9,8},{10,9},{11,1... | collective-permute-start | bytes 165896 | tf_op jit(solution)/shard_map/ppermute | solution.py:23
  144.7 11.1 %collective-permute-done.11 = f32[6,6,1,384]{3,2,1,0:T(1,128)S(1)} collective-permute-done((f32[6,6,1,384]{3,2,1,0:T(1,128)S(1)}, f32[6,6,1,384]{3,2,1,0:T(1,128)S(1)}, u32[]{:S(2)}, u32[]{:S(2)}) %collective-permute-start.11) | collective-permute-done | bytes 55328 | tf_op jit(solution)/shard_map/ppermute | solution.py:23
  157.1 1.6 concatenate.84
  158.6 3.6 %fusion.3 = f32[4,4,32,512]{3,2,1,0:T(8,128)S(1)} fusion(f32[4,4,32,512]{3,2,1,0:T(8,128)} %param.8, f32[4,4,32,512]{3,2,1,0:T(8,128)} %convolution_multiply_fusion, f32[4,4,32,384]{3,2,1,0:T(8,128)S(1)} %concatenate.84, f32[384,512]{1,0:T(8,128)} %param.12), kind=kOutput, calls=%fused_computation.9 | convolution fusion | flops 1208483840 | bytes 4718592 | tf_op jit(solution)/shard_map/dot_general | solution.py:64
  163.4 14.0 %all-gather.1 = f32[8,64,8]{1,2,0:T(8,128)S(1)} all-gather(f32[1,64,8]{1,2,0:T(8,128)S(1)} %convolution_bitcast_fusion), channel_id=1, replica_groups=mesh['gx'=8,'gy'=4,'gz'=32] {'gx'}, dimensions={0}, use_global_device_ids=true | all-gather | bytes 18432 | tf_op jit(solution)/shard_map/all_gather | solution.py:82
  177.5 3.8 %collective-permute-start.12 = (f32[1,1,8,512]{3,2,1,0:T(8,128)S(1)}, f32[1,1,8,512]{3,2,1,0:T(8,128)S(1)}, u32[]{:S(2)}, u32[]{:S(2)}) collective-permute-start(f32[1,1,8,512]{3,2,1,0:T(8,128)S(1)} %fusion.40), channel_id=1, source_target_pairs={{0,32},{32,64},{64,96},{1,33},{33,65},{65,97},{2,34},{34,66},{66,9... | collective-permute-start | bytes 49160 | tf_op jit(solution)/shard_map/ppermute | solution.py:21
  181.3 2.0 %collective-permute-start.13 = (f32[1,1,8,512]{3,2,1,0:T(8,128)S(1)}, f32[1,1,8,512]{3,2,1,0:T(8,128)S(1)}, u32[]{:S(2)}, u32[]{:S(2)}) collective-permute-start(f32[1,1,8,512]{3,2,1,0:T(8,128)S(1)} %fusion.40), channel_id=1, source_target_pairs={{32,0},{64,32},{96,64},{33,1},{65,33},{97,65},{34,2},{66,34},{98,6... | collective-permute-start | bytes 49160 | tf_op jit(solution)/shard_map/ppermute | solution.py:23
  183.6 3.3 %collective-permute-done.13 = f32[1,1,8,512]{3,2,1,0:T(8,128)S(1)} collective-permute-done((f32[1,1,8,512]{3,2,1,0:T(8,128)S(1)}, f32[1,1,8,512]{3,2,1,0:T(8,128)S(1)}, u32[]{:S(2)}, u32[]{:S(2)}) %collective-permute-start.13) | collective-permute-done | bytes 16416 | tf_op jit(solution)/shard_map/ppermute | solution.py:23
  187.0 1.9 collective-permute-start.14
  188.9 3.9 %collective-permute-start.15 = (f32[3,1,8,512]{3,2,1,0:T(8,128)S(1)}, f32[3,1,8,512]{3,2,1,0:T(8,128)S(1)}, u32[]{:S(2)}, u32[]{:S(2)}) collective-permute-start(f32[3,1,8,512]{3,2,1,0:T(8,128)S(1)} %pad_maximum_fusion.52), channel_id=1, source_target_pairs={{1,0},{2,1},{3,2},{4,3},{5,4},{6,5},{7,6},{8,7},{9,8},{10,9},{11,1... | collective-permute-start | bytes 147464 | tf_op jit(solution)/shard_map/ppermute | solution.py:23
  193.0 8.4 %collective-permute-done.15 = f32[3,1,8,512]{3,2,1,0:T(8,128)S(1)} collective-permute-done((f32[3,1,8,512]{3,2,1,0:T(8,128)S(1)}, f32[3,1,8,512]{3,2,1,0:T(8,128)S(1)}, u32[]{:S(2)}, u32[]{:S(2)}) %collective-permute-start.15) | collective-permute-done | bytes 49184 | tf_op jit(solution)/shard_map/ppermute | solution.py:23
  (64 shorter events, 19.3 us)
Async XLA Ops:
  0.0 1.2 copy-start
  4.3 7.2 %copy-start.2 = (f32[4,4,32,512]{3,2,1,0:T(8,128)}, f32[4,4,32,512]{3,2,1,0:T(8,128)S(1)}, u32[]{:S(2)}) copy-start(f32[4,4,32,512]{3,2,1,0:T(8,128)S(1)} %convolution_divide_fusion.1) | copy-start | bytes 3145732
  16.9 15.1 %copy-start.6 = (s32[4,4,32]{2,1,0:T(4,128)S(1)}, s32[4,4,32]{2,1,0:T(4,128)}, u32[]{:S(2)}) copy-start(s32[4,4,32]{2,1,0:T(4,128)} %param.15) | copy-start | bytes 6148
  19.8 41.0 %copy-start.1 = (f32[512,512]{1,0:T(8,128)S(1)}, f32[512,512]{1,0:T(8,128)}, u32[]{:S(2)}) copy-start(f32[512,512]{1,0:T(8,128)} %param.10) | copy-start | bytes 3145732
  19.8 41.0 %copy-start.5 = (f32[4,4,32]{2,1,0:T(4,128)S(1)}, f32[4,4,32]{2,1,0:T(4,128)}, u32[]{:S(2)}) copy-start(f32[4,4,32]{2,1,0:T(4,128)} %param.9) | copy-start | bytes 6148
  29.0 25.9 %collective-permute-start = (f32[1,4,32,384]{3,2,1,0:T(8,128)}, f32[1,4,32,384]{3,2,1,0:T(8,128)S(1)}, u32[]{:S(2)}, u32[]{:S(2)}) collective-permute-start(f32[1,4,32,384]{3,2,1,0:T(8,128)} %get-tuple-element.40), channel_id=1, source_target_pairs={{0,128},{128,256},{256,384},{384,512},{512,640},{640,768},{768,896... | collective-permute-start | bytes 589832 | tf_op jit(solution)/shard_map/ppermute | solution.py:21
  30.7 24.2 %collective-permute-start.1 = (f32[1,4,32,384]{3,2,1,0:T(8,128)S(1)}, f32[1,4,32,384]{3,2,1,0:T(8,128)S(1)}, u32[]{:S(2)}, u32[]{:S(2)}) collective-permute-start(f32[1,4,32,384]{3,2,1,0:T(8,128)S(1)} %get-tuple-element.39), channel_id=1, source_target_pairs={{128,0},{256,128},{384,256},{512,384},{640,512},{768,640},{896,768... | collective-permute-start | bytes 589832 | tf_op jit(solution)/shard_map/ppermute | solution.py:23
  54.9 9.9 %collective-permute-start.3 = (f32[6,1,32,384]{3,2,1,0:T(8,128)S(1)}, f32[6,1,32,384]{3,2,1,0:T(8,128)S(1)}, u32[]{:S(2)}, u32[]{:S(2)}) collective-permute-start(f32[6,1,32,384]{3,2,1,0:T(8,128)S(1)} %get-tuple-element.29), channel_id=1, source_target_pairs={{32,0},{64,32},{96,64},{33,1},{65,33},{97,65},{34,2},{66,34},{98,6... | collective-permute-start | bytes 884744 | tf_op jit(solution)/shard_map/ppermute | solution.py:23
  57.4 8.6 %collective-permute-start.2 = (f32[6,1,32,384]{3,2,1,0:T(8,128)S(1)}, f32[6,1,32,384]{3,2,1,0:T(8,128)S(1)}, u32[]{:S(2)}, u32[]{:S(2)}) collective-permute-start(f32[6,1,32,384]{3,2,1,0:T(8,128)S(1)} %get-tuple-element.30), channel_id=1, source_target_pairs={{0,32},{32,64},{64,96},{1,33},{33,65},{65,97},{2,34},{34,66},{66,9... | collective-permute-start | bytes 884744 | tf_op jit(solution)/shard_map/ppermute | solution.py:21
  64.9 26.9 %copy-start.3 = (f32[4,4,32,512]{3,2,1,0:T(8,128)S(1)}, f32[4,4,32,512]{3,2,1,0:T(8,128)}, u32[]{:S(2)}) copy-start(f32[4,4,32,512]{3,2,1,0:T(8,128)} %convolution_multiply_fusion.1) | copy-start | bytes 3145732
  66.1 13.0 %collective-permute-start.4 = (f32[6,6,1,384]{3,2,1,0:T(1,128)S(1)}, f32[6,6,1,384]{3,2,1,0:T(1,128)S(1)}, u32[]{:S(2)}, u32[]{:S(2)}) collective-permute-start(f32[6,6,1,384]{3,2,1,0:T(1,128)S(1)} %get-tuple-element.24), channel_id=1, source_target_pairs={{0,1},{1,2},{2,3},{3,4},{4,5},{5,6},{6,7},{7,8},{8,9},{9,10},{10,1... | collective-permute-start | bytes 165896 | tf_op jit(solution)/shard_map/ppermute | solution.py:21
  76.2 12.7 %collective-permute-start.5 = (f32[6,6,1,384]{3,2,1,0:T(1,128)S(1)}, f32[6,6,1,384]{3,2,1,0:T(1,128)S(1)}, u32[]{:S(2)}, u32[]{:S(2)}) collective-permute-start(f32[6,6,1,384]{3,2,1,0:T(1,128)S(1)} %get-tuple-element.23), channel_id=1, source_target_pairs={{1,0},{2,1},{3,2},{4,3},{5,4},{6,5},{7,6},{8,7},{9,8},{10,9},{11,1... | collective-permute-start | bytes 165896 | tf_op jit(solution)/shard_map/ppermute | solution.py:23
  120.7 2.7 %collective-permute-start.6 = (f32[1,4,32,384]{3,2,1,0:T(8,128)S(1)}, f32[1,4,32,384]{3,2,1,0:T(8,128)S(1)}, u32[]{:S(2)}, u32[]{:S(2)}) collective-permute-start(f32[1,4,32,384]{3,2,1,0:T(8,128)S(1)} %get-tuple-element.38), channel_id=1, source_target_pairs={{0,128},{128,256},{256,384},{384,512},{512,640},{640,768},{768,896... | collective-permute-start | bytes 589832 | tf_op jit(solution)/shard_map/ppermute | solution.py:21
  122.0 3.3 %collective-permute-start.7 = (f32[1,4,32,384]{3,2,1,0:T(8,128)S(1)}, f32[1,4,32,384]{3,2,1,0:T(8,128)S(1)}, u32[]{:S(2)}, u32[]{:S(2)}) collective-permute-start(f32[1,4,32,384]{3,2,1,0:T(8,128)S(1)} %get-tuple-element.37), channel_id=1, source_target_pairs={{128,0},{256,128},{384,256},{512,384},{640,512},{768,640},{896,768... | collective-permute-start | bytes 589832 | tf_op jit(solution)/shard_map/ppermute | solution.py:23
  125.4 10.4 %collective-permute-start.9 = (f32[6,1,32,384]{3,2,1,0:T(8,128)S(1)}, f32[6,1,32,384]{3,2,1,0:T(8,128)S(1)}, u32[]{:S(2)}, u32[]{:S(2)}) collective-permute-start(f32[6,1,32,384]{3,2,1,0:T(8,128)S(1)} %get-tuple-element.27), channel_id=1, source_target_pairs={{32,0},{64,32},{96,64},{33,1},{65,33},{97,65},{34,2},{66,34},{98,6... | collective-permute-start | bytes 884744 | tf_op jit(solution)/shard_map/ppermute | solution.py:23
  127.4 10.6 %collective-permute-start.8 = (f32[6,1,32,384]{3,2,1,0:T(8,128)S(1)}, f32[6,1,32,384]{3,2,1,0:T(8,128)S(1)}, u32[]{:S(2)}, u32[]{:S(2)}) collective-permute-start(f32[6,1,32,384]{3,2,1,0:T(8,128)S(1)} %get-tuple-element.28), channel_id=1, source_target_pairs={{0,32},{32,64},{64,96},{1,33},{33,65},{65,97},{2,34},{34,66},{66,9... | collective-permute-start | bytes 884744 | tf_op jit(solution)/shard_map/ppermute | solution.py:21
  138.1 6.6 %collective-permute-start.10 = (f32[6,6,1,384]{3,2,1,0:T(1,128)S(1)}, f32[6,6,1,384]{3,2,1,0:T(1,128)S(1)}, u32[]{:S(2)}, u32[]{:S(2)}) collective-permute-start(f32[6,6,1,384]{3,2,1,0:T(1,128)S(1)} %get-tuple-element.20), channel_id=1, source_target_pairs={{0,1},{1,2},{2,3},{3,4},{4,5},{5,6},{6,7},{7,8},{8,9},{9,10},{10,1... | collective-permute-start | bytes 165896 | tf_op jit(solution)/shard_map/ppermute | solution.py:21
  140.1 15.7 %collective-permute-start.11 = (f32[6,6,1,384]{3,2,1,0:T(1,128)S(1)}, f32[6,6,1,384]{3,2,1,0:T(1,128)S(1)}, u32[]{:S(2)}, u32[]{:S(2)}) collective-permute-start(f32[6,6,1,384]{3,2,1,0:T(1,128)S(1)} %get-tuple-element.19), channel_id=1, source_target_pairs={{1,0},{2,1},{3,2},{4,3},{5,4},{6,5},{7,6},{8,7},{9,8},{10,9},{11,1... | collective-permute-start | bytes 165896 | tf_op jit(solution)/shard_map/ppermute | solution.py:23
  157.1 5.2 %copy-start.4 = (f32[512,8]{0,1:T(8,128)S(1)}, f32[512,8]{0,1:T(8,128)}, u32[]{:S(2)}) copy-start(f32[512,8]{0,1:T(8,128)} %param.13) | copy-start | bytes 49156
  157.1 35.8 %copy-start.7 = (f32[8,8]{1,0:T(8,128)S(1)}, f32[8,8]{1,0:T(8,128)}, u32[]{:S(2)}) copy-start(f32[8,8]{1,0:T(8,128)} %param.14) | copy-start | bytes 772
  177.5 6.1 %collective-permute-start.12 = (f32[1,1,8,512]{3,2,1,0:T(8,128)S(1)}, f32[1,1,8,512]{3,2,1,0:T(8,128)S(1)}, u32[]{:S(2)}, u32[]{:S(2)}) collective-permute-start(f32[1,1,8,512]{3,2,1,0:T(8,128)S(1)} %fusion.40), channel_id=1, source_target_pairs={{0,32},{32,64},{64,96},{1,33},{33,65},{65,97},{2,34},{34,66},{66,9... | collective-permute-start | bytes 49160 | tf_op jit(solution)/shard_map/ppermute | solution.py:21
  181.3 5.6 %collective-permute-start.13 = (f32[1,1,8,512]{3,2,1,0:T(8,128)S(1)}, f32[1,1,8,512]{3,2,1,0:T(8,128)S(1)}, u32[]{:S(2)}, u32[]{:S(2)}) collective-permute-start(f32[1,1,8,512]{3,2,1,0:T(8,128)S(1)} %fusion.40), channel_id=1, source_target_pairs={{32,0},{64,32},{96,64},{33,1},{65,33},{97,65},{34,2},{66,34},{98,6... | collective-permute-start | bytes 49160 | tf_op jit(solution)/shard_map/ppermute | solution.py:23
  187.0 6.1 %collective-permute-start.14 = (f32[3,1,8,512]{3,2,1,0:T(8,128)S(1)}, f32[3,1,8,512]{3,2,1,0:T(8,128)S(1)}, u32[]{:S(2)}, u32[]{:S(2)}) collective-permute-start(f32[3,1,8,512]{3,2,1,0:T(8,128)S(1)} %pad_maximum_fusion.52), channel_id=1, source_target_pairs={{0,1},{1,2},{2,3},{3,4},{4,5},{5,6},{6,7},{7,8},{8,9},{9,10},{10,1... | collective-permute-start | bytes 147464 | tf_op jit(solution)/shard_map/ppermute | solution.py:21
  188.9 12.6 %collective-permute-start.15 = (f32[3,1,8,512]{3,2,1,0:T(8,128)S(1)}, f32[3,1,8,512]{3,2,1,0:T(8,128)S(1)}, u32[]{:S(2)}, u32[]{:S(2)}) collective-permute-start(f32[3,1,8,512]{3,2,1,0:T(8,128)S(1)} %pad_maximum_fusion.52), channel_id=1, source_target_pairs={{1,0},{2,1},{3,2},{4,3},{5,4},{6,5},{7,6},{8,7},{9,8},{10,9},{11,1... | collective-permute-start | bytes 147464 | tf_op jit(solution)/shard_map/ppermute | solution.py:23
where the time goes:
time: 205 us; the launch traced here: 204 us
  local copies, waits for them, and re-layouts  53.5 us (26%)
  starting transfers between devices  47 us (23%)
  waiting for transfers between devices  39.2 us (19%)
  blocking collectives  34.5 us (17%)
  matrix products  23.7 us (12%)
  other arithmetic  4.98 us (2%)
    ppermute x8, waiting for transfers between devices, extended(): lax.ppermute(head, axis, [((i + 1) % count, i) for i in range(ends)])  35.2 us
    ppermute x8, starting transfers between devices, extended(): lax.ppermute(tail, axis, [(i, (i + 1) % count) for i in range(ends)])  28.1 us
    another operation x16, local copies, waits for them, and re-layouts, face_traces(): return jnp.concatenate([p.reshape(lead + (FACE,)) for p in parts], -1)  27.6 us
    dot_general x11, matrix products, mult(): return jnp.matmul(a, b, precision=high)  23.7 us
    unnamed x1, blocking collectives  20.5 us
    ppermute x8, starting transfers between devices, extended(): lax.ppermute(head, axis, [((i + 1) % count, i) for i in range(ends)])  18.9 us
    all_gather x1, blocking collectives, shards(): lax.all_gather(local_rhs, 'gx', axis=1, tiled=True)  14 us
    slice x2, local copies, waits for them, and re-layouts, face_traces(): cube[..., :, :, last]  10 us
  transfers between devices with their start and end apart: 16, of which 9 were waited for; matrix products, arithmetic and copies ran while one was open for 5% of the time, Pallas kernels for 0%

commit v1 on v0

v1 whole, which is shorter than its diff:
```python
import functools

import jax
import jax.numpy as jnp
from jax import lax
from jax.experimental import pallas as pl
from jax.experimental.pallas import tpu as pltpu
from jax.sharding import PartitionSpec as P

N = 512
FACE = 64
F32 = jnp.float32
BF16 = jnp.bfloat16
MESH = pl.DeviceIdType.MESH
NT = (((1,), (1,)), ((), ()))
TN = (((0,), (0,)), ((), ()))
NN = (((1,), (0,)), ((), ()))


def dot3(a, b, dims=NN):
    return lax.dot_general(a, b, dims, precision=lax.Precision.HIGH, preferred_element_type=F32)


def halves(a):
    hi = a.astype(BF16)
    return hi, (a - hi.astype(F32)).astype(BF16)


def dot1(a, b):
    return jnp.dot(a, b, preferred_element_type=F32)


def iota(shape, dim):
    return lax.broadcasted_iota(jnp.int32, shape, dim)


def kernel(
    sizes, rhs_hbm, coef_hbm, mass_hbm, smoother_hbm, lift_hbm, restrict_hbm, cbm_hbm, label_hbm,
    out_ref,
    rhs, mass, smoother, lift, restrict, cbm, coef, label,
    dcol, onehot, pick, u, first, tr, faces, big, ls, lsg, g, x_t,
    out_a, in_a, out_z, in_z, in_bx, in_by, in_bz, zone_out, in_zone,
    load_sem, sa, ra, sb, rb, sz, rz,
):
    ngx, ngy, ngz = sizes
    gx, gy, gz = lax.axis_index("gx"), lax.axis_index("gy"), lax.axis_index("gz")

    loads = [
        pltpu.make_async_copy(src, dst, load_sem.at[n])
        for n, (src, dst) in enumerate(
            [
                (rhs_hbm, rhs),
                (smoother_hbm, smoother),
                (coef_hbm, coef),
                (label_hbm, label),
                (restrict_hbm, restrict),
                (cbm_hbm, cbm),
                (mass_hbm, mass),
                (lift_hbm.at[FACE : 2 * FACE], lift.at[0:FACE]),
                (lift_hbm.at[0:FACE], lift.at[FACE : 2 * FACE]),
                (lift_hbm.at[2 * FACE :], lift.at[2 * FACE :]),
            ]
        )
    ]
    for copy in loads:
        copy.start()

    def along(axis, place, size, step):
        return {axis: lax.rem(place + (step + size), size)}

    down = [along("gx", gx, ngx, -1), along("gy", gy, ngy, -1), along("gz", gz, ngz, -1)]
    up = [along("gx", gx, ngx, 1), along("gy", gy, ngy, 1), along("gz", gz, ngz, 1)]
    line = [along("gx", gx, ngx, step) for step in range(1, ngx)]

    barrier = pltpu.get_barrier_semaphore()
    partners = line + down[1:] + up[1:]
    for partner in partners:
        pl.semaphore_signal(barrier, inc=1, device_id=partner, device_id_type=MESH)

    node, face = iota((N, 256), 0), iota((N, 256), 1)
    block, within = face // FACE, face % FACE
    hi, lo = within // 8, within % 8
    end = jnp.where(block % 2 == 0, 7, 0)
    wanted = jnp.where(block < 2, hi * 64 + end * 8 + lo, hi * 64 + lo * 8 + end)
    pick[...] = jnp.where(node == wanted, 1.0, 0.0).astype(BF16)

    lane = iota((32, 128), 1)
    row = iota((32, 128), 0)

    def column(values):
        return jnp.sum(jnp.where(lane == row, jnp.broadcast_to(values, (32, 128)), 0.0), 1, keepdims=True)

    loads[2].wait()
    loads[3].wait()
    pad = jnp.zeros((1, 96), F32)
    for s in range(16):
        values = jnp.concatenate([coef[s // 4, s % 4 : s % 4 + 1, :], pad], 1)
        dcol[32 * s : 32 * s + 32, :] = jnp.broadcast_to(1.0 / column(values), (32, 128))
        names = jnp.concatenate([label[s // 4, s % 4 : s % 4 + 1, :].astype(F32), pad], 1)
        names = jnp.broadcast_to(column(names), (32, 128)).astype(jnp.int32)
        onehot[32 * s : 32 * s + 32, :] = jnp.where(names == lane, 1.0, 0.0)
    d4 = lambda a: jnp.concatenate([a] * 4, 1)

    loads[0].wait()
    loads[1].wait()
    u[...] = dot3(rhs[...], smoother[...])
    first[...] = u[...] * d4(dcol[...])
    f_hi, f_lo = halves(first[...])
    tr[...] = dot1(f_hi, pick[...]) + dot1(f_lo, pick[...])

    low = iota((FACE, 128), 1) < FACE
    swap = lambda a: pltpu.roll(a, FACE, 1)
    top, bottom = first[384:512, 384:512], first[0:128, 0:128]
    out_a[0] = jnp.where(low, swap(top[0:64]), top[64:128])
    out_a[1] = jnp.where(low, bottom[0:64], swap(bottom[64:128]))
    ytop = [tr[128 * i + 96 : 128 * i + 128, 0:128] for i in range(4)]
    ybottom = [tr[128 * i : 128 * i + 32, 0:128] for i in range(4)]
    out_a[2] = jnp.where(low, jnp.concatenate(ytop[:2], 0), swap(jnp.concatenate(ytop[2:], 0)))
    out_a[3] = jnp.where(low, swap(jnp.concatenate(ybottom[:2], 0)), jnp.concatenate(ybottom[2:], 0))
    for s in range(16):
        out_z[0, s : s + 1, :] = tr[32 * s + 31 : 32 * s + 32, 128:256]
        out_z[1, s : s + 1, :] = tr[32 * s : 32 * s + 1, 128:256]

    pl.semaphore_wait(barrier, len(partners))

    def send(src, dst, send_sem, recv_sem, device):
        copy = pltpu.make_async_remote_copy(
            src_ref=src, dst_ref=dst, send_sem=send_sem, recv_sem=recv_sem,
            device_id=device, device_id_type=MESH,
        )
        copy.start()
        return copy

    a_copies = []
    for dim in range(3):
        for way, device in enumerate((up[dim], down[dim])):
            n = 2 * dim + way
            src, dst = (out_a.at[n], in_a.at[n]) if dim < 2 else (out_z.at[way], in_z.at[way])
            a_copies.append(send(src, dst, sa.at[n], ra.at[n], device))

    low32 = lane < FACE
    nothing = jnp.zeros((32, 128), F32)
    for s in range(16):
        x, y = s // 4, s % 4
        rows = slice(32 * s, 32 * s + 32)
        above = first[32 * s + 128 : 32 * s + 160, 0:128] if x < 3 else nothing
        below = first[32 * s - 128 : 32 * s - 96, 384:512] if x > 0 else nothing
        faces[rows, 0:128] = jnp.where(low32, above, below)
        above = tr[32 * s + 32 : 32 * s + 64, 0:128] if y < 3 else nothing
        below = tr[32 * s - 32 : 32 * s, 0:128] if y > 0 else nothing
        faces[rows, 128:256] = jnp.where(low32, below, above)
        own = tr[rows, 128:256]
        below = jnp.where(row == 0, 0.0, pltpu.roll(own, 1, 0))
        above = jnp.where(row == 31, 0.0, pltpu.roll(own, 31, 0))
        faces[rows, 256:384] = jnp.where(low32, below, above)

    for copy in loads[4:]:
        copy.wait()

    many = jnp.concatenate([restrict[...]] * 16, 0)
    lane_n = iota((N, 128), 1)
    lift_r = dot3(lift[...], many, NT)
    face_row = iota((384, 128), 0) // FACE
    lift_r = jnp.where(iota((384, 128), 1) // 8 == face_row + 1, lift_r, 0.0)
    g_now = jnp.where(lane_n < 8, dot3(mass[...], many, NT), 0.0)
    l_hi, l_lo = halves(lift_r[128:384])
    g_now = g_now + (dot1(pick[...], l_hi) + dot1(pick[...], l_lo))
    g[...] = g_now
    g[0:64, :] = g[0:64, :] + lift_r[0:64]
    g[448:512, :] = g[448:512, :] + lift_r[64:128]
    ls[...] = dot3(lift[...], smoother[...])
    lsg[...] = dot3(ls[...], g[...])
    rr = dot3(rhs[...], many, NT)

    big[...] = rhs[...] - dot3(u[...], mass[...]) + dot3(faces[...], lift[...])
    u[...] = u[...] + dot3(big[...], smoother[...])
    w = dot3(u[...], g[...])
    x_t[...] = w

    for copy in a_copies:
        copy.wait_recv()
    is_in = [
        jnp.where(gx > 0, 1.0, 0.0), jnp.where(gx < ngx - 1, 1.0, 0.0),
        jnp.where(gy > 0, 1.0, 0.0), jnp.where(gy < ngy - 1, 1.0, 0.0),
        jnp.where(gz > 0, 1.0, 0.0), jnp.where(gz < ngz - 1, 1.0, 0.0),
    ]
    halo_rows = []
    for n in range(4):
        packed = in_a[n] * is_in[n]
        halo = jnp.concatenate([packed, swap(packed)], 0)[:, 0:FACE]
        at = {0: 64, 1: 0, 2: 128, 3: 192}[n]
        halo_rows.append((n, halo, at))
        add = dot3(halo, lsg[at : at + FACE, :])
        if n == 0:
            x_t[0:128, :] = x_t[0:128, :] + add
        elif n == 1:
            x_t[384:512, :] = x_t[384:512, :] + add
        else:
            for i in range(4):
                j = 128 * i + (0 if n == 2 else 96)
                x_t[j : j + 32, :] = x_t[j : j + 32, :] + add[32 * i : 32 * i + 32]
    z_low = in_z[0] * is_in[4]
    z_high = in_z[1] * is_in[5]
    add_low = dot3(z_low[:, 0:FACE], lsg[256:320, :])
    add_high = dot3(z_high[:, FACE:128], lsg[320:384, :])
    for s in range(16):
        x_t[32 * s : 32 * s + 1, :] = x_t[32 * s : 32 * s + 1, :] + add_low[s : s + 1]
        x_t[32 * s + 31 : 32 * s + 32, :] = x_t[32 * s + 31 : 32 * s + 32, :] + add_high[s : s + 1]

    w = x_t[...]
    w = jnp.where(lane_n < 8, rr - w, w * dcol[...])
    c = big
    c[0:128, :] = w.T

    b_copies = [
        send(c.at[16:24, 384:512], in_bx.at[0], sb.at[0], rb.at[0], up[0]),
        send(c.at[8:16, 0:128], in_bx.at[1], sb.at[1], rb.at[1], down[0]),
        send(c.at[24:32, :], in_by.at[0], sb.at[2], rb.at[2], up[1]),
        send(c.at[32:40, :], in_by.at[1], sb.at[3], rb.at[3], down[1]),
        send(c.at[40:48, :], in_bz.at[0], sb.at[4], rb.at[4], up[2]),
        send(c.at[48:56, :], in_bz.at[1], sb.at[5], rb.at[5], down[2]),
    ]

    small = c[0:8, :]
    none8 = jnp.zeros((8, 128), F32)
    place = iota((8, N), 1)
    py, pz = (place // 32) % 4, place % 32
    small = small + jnp.concatenate([c[8:16, 128:512], none8], 1)
    small = small + jnp.concatenate([none8, c[16:24, 0:384]], 1)
    small = small + jnp.where(py > 0, pltpu.roll(c[24:32, :], 32, 1), 0.0)
    small = small + jnp.where(py < 3, pltpu.roll(c[32:40, :], N - 32, 1), 0.0)
    small = small + jnp.where(pz > 0, pltpu.roll(c[40:48, :], 1, 1), 0.0)
    small = small + jnp.where(pz < 31, pltpu.roll(c[48:56, :], N - 1, 1), 0.0)
    weight = 1.0 + jnp.sum(onehot[...], 0, keepdims=True)
    weight = jnp.broadcast_to(weight, (8, 128))

    for copy in b_copies:
        copy.wait_recv()
    zeros_mid = jnp.zeros((8, 256), F32)
    small = small + jnp.concatenate([in_bx[0] * is_in[0], zeros_mid, in_bx[1] * is_in[1]], 1)
    small = small + jnp.where(py == 0, pltpu.roll(in_by[0], N - 96, 1) * is_in[2], 0.0)
    small = small + jnp.where(py == 3, pltpu.roll(in_by[1], 96, 1) * is_in[3], 0.0)
    small = small + jnp.where(pz == 0, pltpu.roll(in_bz[0], N - 31, 1) * is_in[4], 0.0)
    small = small + jnp.where(pz == 31, pltpu.roll(in_bz[1], 31, 1) * is_in[5], 0.0)
    coarse_rhs = dot3(small, onehot[...])
    zone = coarse_rhs / weight
    zone_out[...] = zone

    z_copies = []
    for n, device in enumerate(line + [up[1], down[1], up[2], down[2]]):
        z_copies.append(send(zone_out, in_zone.at[n], sz.at[n], rz.at[n], device))

    add_low = dot3(z_low[:, 0:FACE], ls[256:320, :])
    add_high = dot3(z_high[:, FACE:128], ls[320:384, :])
    for s in range(16):
        u[32 * s : 32 * s + 1, :] = u[32 * s : 32 * s + 1, :] + add_low[s : s + 1]
        u[32 * s + 31 : 32 * s + 32, :] = u[32 * s + 31 : 32 * s + 32, :] + add_high[s : s + 1]
    for n, halo, at in halo_rows:
        add = dot3(halo, ls[at : at + FACE, :])
        if n == 0:
            u[0:128, :] = u[0:128, :] + add
        elif n == 1:
            u[384:512, :] = u[384:512, :] + add
        else:
            for i in range(4):
                j = 128 * i + (0 if n == 2 else 96)
                u[j : j + 32, :] = u[j : j + 32, :] + add[32 * i : 32 * i + 32]
    u[...] = u[...] * d4(dcol[...])
    inner = weight * dot3(cbm[...], zone)

    for copy in z_copies:
        copy.wait_recv()
    total = zone
    for n in range(ngx - 1):
        total = total + in_zone[n]
    k = ngx - 1
    total = total + (in_zone[k] * is_in[2] + in_zone[k + 1] * is_in[3] + in_zone[k + 2] * is_in[4] + in_zone[k + 3] * is_in[5])
    two = zone + (coarse_rhs - (inner - total)) / weight
    spread = dot3(two, restrict[...], TN)
    s_hi, s_lo = halves(spread)
    one = onehot[...].astype(BF16)
    out_ref[...] = u[...] + (dot1(one, s_hi) + dot1(one, s_lo))

    for copy in a_copies + b_copies + z_copies:
        copy.wait_send()


def shards(sizes, rhs, coef, mass, smoother, lift, restrict, coarse_block_matrix, element_cluster_index):
    others = sizes[0] - 1 + 4
    hbm = pl.BlockSpec(memory_space=pl.ANY)
    dma = pltpu.SemaphoreType.DMA
    out = pl.pallas_call(
        functools.partial(kernel, sizes),
        out_shape=jax.ShapeDtypeStruct((N, N), F32),
        in_specs=[hbm] * 8,
        out_specs=pl.BlockSpec(memory_space=pltpu.VMEM),
        scratch_shapes=[
            pltpu.VMEM((N, N), F32),
            pltpu.VMEM((N, N), F32),
            pltpu.VMEM((N, N), F32),
            pltpu.VMEM((384, N), F32),
            pltpu.VMEM((8, N), F32),
            pltpu.VMEM((8, 8), F32),
            pltpu.VMEM((4, 4, 32), F32),
            pltpu.VMEM((4, 4, 32), jnp.int32),
            pltpu.VMEM((N, 128), F32),
            pltpu.VMEM((N, 128), F32),
            pltpu.VMEM((N, 256), BF16),
            pltpu.VMEM((N, N), F32),
            pltpu.VMEM((N, N), F32),
            pltpu.VMEM((N, 256), F32),
            pltpu.VMEM((N, 384), F32),
            pltpu.VMEM((N, N), F32),
            pltpu.VMEM((384, N), F32),
            pltpu.VMEM((384, 128), F32),
            pltpu.VMEM((N, 128), F32),
            pltpu.VMEM((N, 128), F32),
            pltpu.VMEM((4, 64, 128), F32),
            pltpu.VMEM((4, 64, 128), F32),
            pltpu.VMEM((2, 16, 128), F32),
            pltpu.VMEM((2, 16, 128), F32),
            pltpu.VMEM((2, 8, 128), F32),
            pltpu.VMEM((2, 8, N), F32),
            pltpu.VMEM((2, 8, N), F32),
            pltpu.VMEM((8, 128), F32),
            pltpu.VMEM((others, 8, 128), F32),
            dma((10,)),
            dma((6,)),
            dma((6,)),
            dma((6,)),
            dma((6,)),
            dma((others,)),
            dma((others,)),
        ],
        compiler_params=pltpu.CompilerParams(
            collective_id=0, has_side_effects=True, vmem_limit_bytes=40 * 1024 * 1024
        ),
        name="cycle",
    )(rhs.reshape(N, N), coef, mass, smoother, lift, restrict.T, coarse_block_matrix, element_cluster_index)
    return out.reshape(rhs.shape)


def solution(mesh):
    sizes = tuple(mesh.shape[a] for a in ("gx", "gy", "gz"))
    return jax.shard_map(
        functools.partial(shards, sizes),
        mesh=mesh,
        in_specs=(
            P("gx", "gy", "gz", None),
            P("gx", "gy", "gz"),
            P(),
            P(),
            P(),
            P(),
            P(),
            P("gx", "gy", "gz"),
        ),
        out_specs=P("gx", "gy", "gz", None),
        check_vma=False,
    )
```

time: 205 us -> 49.8 us (0.24)
  the two profiles are of different devices: /device:TPU:58 before, /device:TPU:1 now
where the time goes in v1:
time: 49.8 us; the launch traced here: 49.3 us
  Pallas kernels  40.7 us (82%)
  local copies, waits for them, and re-layouts  8.57 us (17%)
    pallas_call x1, Pallas kernels, shards(): pl.pallas_call(functools.partial(kernel, sizes), out_shape=jax.ShapeDtype...  40.7 us
    unnamed x17, local copies, waits for them, and re-layouts  8.57 us

profile of v1, /device:TPU:1, one launch (start us, length us, event | category | flops | bytes accessed | tf_op | source)
XLA Modules:
  0.0 49.3 jit_solution(2359604495144930086)
XLA Ops:
  0.0 0.0 copy-start
  0.0 1.2 %copy-done = f32[4,4,32,512]{3,2,1,0:T(8,128)S(1)} copy-done((f32[4,4,32,512]{3,2,1,0:T(8,128)S(1)}, f32[4,4,32,512]{3,2,1,0:T(8,128)}, u32[]{:S(2)}) %copy-start) | copy-done | bytes 1048600
  1.2 0.0 copy-start.1
  1.2 1.2 %copy-done.1 = f32[512,512]{1,0:T(8,128)S(1)} copy-done((f32[512,512]{1,0:T(8,128)S(1)}, f32[512,512]{1,0:T(8,128)}, u32[]{:S(2)}) %copy-start.1) | copy-done | bytes 1048600
  2.5 0.0 copy-start.2
  2.5 1.2 %copy-done.2 = f32[512,512]{1,0:T(8,128)S(1)} copy-done((f32[512,512]{1,0:T(8,128)S(1)}, f32[512,512]{1,0:T(8,128)}, u32[]{:S(2)}) %copy-start.2) | copy-done | bytes 1048600
  3.7 0.0 copy-start.3
  3.7 1.1 %copy-done.3 = f32[384,512]{1,0:T(8,128)S(1)} copy-done((f32[384,512]{1,0:T(8,128)S(1)}, f32[384,512]{1,0:T(8,128)}, u32[]{:S(2)}) %copy-start.3) | copy-done | bytes 786456
  4.8 0.0 copy-start.4
  4.8 0.7 %copy-done.4 = f32[512,8]{0,1:T(8,128)S(1)} copy-done((f32[512,8]{0,1:T(8,128)S(1)}, f32[512,8]{0,1:T(8,128)}, u32[]{:S(2)}) %copy-start.4) | copy-done | bytes 16408
  5.5 0.0 copy-start.5
  5.5 0.7 %copy-done.5 = f32[4,4,32]{2,1,0:T(4,128)S(1)} copy-done((f32[4,4,32]{2,1,0:T(4,128)S(1)}, f32[4,4,32]{2,1,0:T(4,128)}, u32[]{:S(2)}) %copy-start.5) | copy-done | bytes 2072
  6.2 0.0 copy-start.6
  6.2 0.7 %copy-done.6 = s32[4,4,32]{2,1,0:T(4,128)S(1)} copy-done((s32[4,4,32]{2,1,0:T(4,128)S(1)}, s32[4,4,32]{2,1,0:T(4,128)}, u32[]{:S(2)}) %copy-start.6) | copy-done | bytes 2072
  6.9 0.0 copy-start.7
  6.9 0.7 %copy-done.7 = f32[8,8]{1,0:T(8,128)S(1)} copy-done((f32[8,8]{1,0:T(8,128)S(1)}, f32[8,8]{1,0:T(8,128)}, u32[]{:S(2)}) %copy-start.7) | copy-done | bytes 280
  7.6 40.7 %cycle.1 = f32[512,512]{1,0:T(8,128)S(1)} custom-call(f32[512,512]{1,0:T(8,128)S(1)} %bitcast.4, f32[4,4,32]{2,1,0:T(4,128)S(1)} %copy-done.5, f32[512,512]{1,0:T(8,128)S(1)} %copy-done.1, f32[512,512]{1,0:T(8,128)S(1)} %copy-done.2, f32[384,512]{1,0:T(8,128)S(1)} %copy-done.3, f32[8,512]{1,0:T(8,128)S(1)} %bitcast.5, f32[8,8]{1,0:T(8,128)S(1)} %copy-done.7, ...), custom_call_target="tpu_custom_call" | custom-call | tf_op jit(solution)/shard_map/cycle/pallas_call | solution.py:292
  48.3 1.0 %copy.10 = f32[4,4,32,512]{3,2,1,0:T(8,128)} copy(f32[4,4,32,512]{3,2,1,0:T(8,128)S(1)} %bitcast.3) | data formatting | bytes 2097152
Async XLA Ops:
  0.0 1.2 %copy-start = (f32[4,4,32,512]{3,2,1,0:T(8,128)S(1)}, f32[4,4,32,512]{3,2,1,0:T(8,128)}, u32[]{:S(2)}) copy-start(f32[4,4,32,512]{3,2,1,0:T(8,128)} %param.8) | copy-start | bytes 3145732
  1.2 1.2 %copy-start.1 = (f32[512,512]{1,0:T(8,128)S(1)}, f32[512,512]{1,0:T(8,128)}, u32[]{:S(2)}) copy-start(f32[512,512]{1,0:T(8,128)} %mass_hbm.1) | copy-start | bytes 3145732
  2.5 1.2 %copy-start.2 = (f32[512,512]{1,0:T(8,128)S(1)}, f32[512,512]{1,0:T(8,128)}, u32[]{:S(2)}) copy-start(f32[512,512]{1,0:T(8,128)} %smoother_hbm.1) | copy-start | bytes 3145732
  3.7 1.1 %copy-start.3 = (f32[384,512]{1,0:T(8,128)S(1)}, f32[384,512]{1,0:T(8,128)}, u32[]{:S(2)}) copy-start(f32[384,512]{1,0:T(8,128)} %lift_hbm.1) | copy-start | bytes 2359300
  4.8 0.7 %copy-start.4 = (f32[512,8]{0,1:T(8,128)S(1)}, f32[512,8]{0,1:T(8,128)}, u32[]{:S(2)}) copy-start(f32[512,8]{0,1:T(8,128)} %param.13) | copy-start | bytes 49156
  5.5 0.7 %copy-start.5 = (f32[4,4,32]{2,1,0:T(4,128)S(1)}, f32[4,4,32]{2,1,0:T(4,128)}, u32[]{:S(2)}) copy-start(f32[4,4,32]{2,1,0:T(4,128)} %coef_hbm.1) | copy-start | bytes 6148
  6.2 0.7 %copy-start.6 = (s32[4,4,32]{2,1,0:T(4,128)S(1)}, s32[4,4,32]{2,1,0:T(4,128)}, u32[]{:S(2)}) copy-start(s32[4,4,32]{2,1,0:T(4,128)} %label_hbm.1) | copy-start | bytes 6148
  6.9 0.7 %copy-start.7 = (f32[8,8]{1,0:T(8,128)S(1)}, f32[8,8]{1,0:T(8,128)}, u32[]{:S(2)}) copy-start(f32[8,8]{1,0:T(8,128)} %cbm_hbm.1) | copy-start | bytes 772

commit v2 on v1

v2 whole, which is shorter than its diff:
```python
import functools

import jax
import jax.numpy as jnp
from jax import lax
from jax.experimental import pallas as pl
from jax.experimental.pallas import tpu as pltpu
from jax.sharding import PartitionSpec as P

N = 512
FACE = 64
F32 = jnp.float32
BF16 = jnp.bfloat16
MESH = pl.DeviceIdType.MESH
NT = (((1,), (1,)), ((), ()))
TN = (((0,), (0,)), ((), ()))
NN = (((1,), (0,)), ((), ()))


def dot3(a, b, dims=NN):
    return lax.dot_general(a, b, dims, precision=lax.Precision.HIGH, preferred_element_type=F32)


def halves(a):
    hi = a.astype(BF16)
    return hi, (a - hi.astype(F32)).astype(BF16)


def dot1(a, b):
    return jnp.dot(a, b, preferred_element_type=F32)


def iota(shape, dim):
    return lax.broadcasted_iota(jnp.int32, shape, dim)


def kernel(
    sizes, rhs_hbm, coef_hbm, mass_hbm, smoother_hbm, lift_hbm, restrict_hbm, cbm_hbm, label_hbm,
    out_ref,
    rhs, mass, smoother, lift, restrict, cbm, coef, label,
    dcol, onehot, pick, u, first, tr, faces, v, g_cat, g_top,
    out_a, in_a, out_z, in_z, c, in_bx, in_by, in_bz, zone_out, in_zone,
    load_sem, sa, ra, sb, rb, sz, rz,
):
    ngx, ngy, ngz = sizes
    places = [lax.axis_index(axis) for axis in ("gx", "gy", "gz")]

    loads = [
        pltpu.make_async_copy(src, dst, load_sem.at[n])
        for n, (src, dst) in enumerate(
            [
                (coef_hbm, coef),
                (label_hbm, label),
                (rhs_hbm, rhs),
                (smoother_hbm, smoother),
                (restrict_hbm, restrict),
                (cbm_hbm, cbm),
                (mass_hbm, mass),
                (lift_hbm.at[FACE : 2 * FACE], lift.at[0:FACE]),
                (lift_hbm.at[0:FACE], lift.at[FACE : 2 * FACE]),
                (lift_hbm.at[2 * FACE :], lift.at[2 * FACE :]),
            ]
        )
    ]
    for copy in loads:
        copy.start()

    def along(dim, step):
        size = sizes[dim]
        return {("gx", "gy", "gz")[dim]: lax.rem(places[dim] + (step + size), size)}

    beside = [(along(dim, 1), along(dim, -1)) for dim in range(3)]
    there = [(places[dim] < sizes[dim] - 1, places[dim] > 0) for dim in range(3)]
    line = [along(0, step) for step in range(1, ngx)]

    barrier = pltpu.get_barrier_semaphore()
    for device in line:
        pl.semaphore_signal(barrier, inc=1, device_id=device, device_id_type=MESH)
    partners = ngx - 1
    for dim in (1, 2):
        for way in (0, 1):
            partners = partners + jnp.where(there[dim][way], 1, 0)

            @pl.when(there[dim][way])
            def _():
                pl.semaphore_signal(barrier, inc=1, device_id=beside[dim][way], device_id_type=MESH)

    class Message:
        def __init__(self, src, dst, send_sem, recv_sem, device, goes, comes):
            self.copy = pltpu.make_async_remote_copy(
                src_ref=src, dst_ref=dst, send_sem=send_sem, recv_sem=recv_sem,
                device_id=device, device_id_type=MESH,
            )
            self.goes, self.comes = goes, comes

        def start(self):
            self.when(self.goes, self.copy.start)
            return self

        def wait_recv(self):
            self.when(self.comes, self.copy.wait_recv)

        def wait_send(self):
            self.when(self.goes, self.copy.wait_send)

        def when(self, condition, act):
            if condition is None:
                act()
            else:
                pl.when(condition)(act)

    def shifted(dim, way, src, dst, send_sem, recv_sem):
        return Message(src, dst, send_sem, recv_sem, beside[dim][way], there[dim][way], there[dim][1 - way])

    for dim in range(3):
        for way in (0, 1):

            @pl.when(jnp.logical_not(there[dim][1 - way]))
            def _():
                if dim < 2:
                    in_a[2 * dim + way] = jnp.zeros((FACE, 128), F32)
                else:
                    in_z[way] = jnp.zeros((16, 128), F32)
                if dim == 0:
                    in_bx[way] = jnp.zeros((8, 128), F32)
                elif dim == 1:
                    in_by[way] = jnp.zeros((8, N), F32)
                else:
                    in_bz[way] = jnp.zeros((8, N), F32)
                if dim > 0:
                    in_zone[ngx - 1 + 2 * (dim - 1) + way] = jnp.zeros((8, 128), F32)

    node, face = iota((N, 256), 0), iota((N, 256), 1)
    block, within = face // FACE, face % FACE
    hi, lo = within // 8, within % 8
    end = jnp.where(block % 2 == 0, 7, 0)
    wanted = jnp.where(block < 2, hi * 64 + end * 8 + lo, hi * 64 + lo * 8 + end)
    pick[...] = jnp.where(node == wanted, 1.0, 0.0).astype(BF16)

    lane = iota((32, 128), 1)
    row = iota((32, 128), 0)

    def column(values):
        return jnp.sum(jnp.where(lane == row, jnp.broadcast_to(values, (32, 128)), 0.0), 1, keepdims=True)

    loads[0].wait()
    loads[1].wait()
    pad = jnp.zeros((1, 96), F32)
    for s in range(16):
        values = jnp.concatenate([coef[s // 4, s % 4 : s % 4 + 1, :], pad], 1)
        dcol[32 * s : 32 * s + 32, :] = jnp.broadcast_to(1.0 / column(values), (32, 128))
        names = jnp.concatenate([label[s // 4, s % 4 : s % 4 + 1, :].astype(F32), pad], 1)
        names = jnp.broadcast_to(column(names), (32, 128)).astype(jnp.int32)
        onehot[32 * s : 32 * s + 32, :] = jnp.where(names == lane % 64, 1.0, 0.0)
    d4 = lambda a: jnp.concatenate([a] * 4, 1)

    loads[2].wait()
    loads[3].wait()
    u[...] = dot3(rhs[...], smoother[...])
    first[...] = u[...] * d4(dcol[...])

    low = iota((FACE, 128), 1) < FACE
    swap = lambda a: pltpu.roll(a, FACE, 1)
    top, bottom = first[384:512, 384:512], first[0:128, 0:128]
    out_a[0] = jnp.where(low, swap(top[0:64]), top[64:128])
    out_a[1] = jnp.where(low, bottom[0:64], swap(bottom[64:128]))
    pl.semaphore_wait(barrier, partners)
    a_copies = [
        shifted(0, way, out_a.at[way], in_a.at[way], sa.at[way], ra.at[way]).start() for way in (0, 1)
    ]

    f_hi, f_lo = halves(first[...])
    tr[...] = dot1(f_hi, pick[...]) + dot1(f_lo, pick[...])
    ytop = [tr[128 * i + 96 : 128 * i + 128, 0:128] for i in range(4)]
    ybottom = [tr[128 * i : 128 * i + 32, 0:128] for i in range(4)]
    out_a[2] = jnp.where(low, jnp.concatenate(ytop[:2], 0), swap(jnp.concatenate(ytop[2:], 0)))
    out_a[3] = jnp.where(low, swap(jnp.concatenate(ybottom[:2], 0)), jnp.concatenate(ybottom[2:], 0))
    for s in range(16):
        out_z[0, s : s + 1, :] = tr[32 * s + 31 : 32 * s + 32, 128:256]
        out_z[1, s : s + 1, :] = tr[32 * s : 32 * s + 1, 128:256]
    a_copies += [
        shifted(1, way, out_a.at[2 + way], in_a.at[2 + way], sa.at[2 + way], ra.at[2 + way]).start()
        for way in (0, 1)
    ]
    a_copies += [
        shifted(2, way, out_z.at[way], in_z.at[way], sa.at[4 + way], ra.at[4 + way]).start()
        for way in (0, 1)
    ]

    for copy in loads[4:]:
        copy.wait()

    v[...] = rhs[...] - dot3(u[...], mass[...])

    many = jnp.concatenate([restrict[...]] * 16, 0)
    lane_n = iota((N, 128), 1)
    first_half = lane_n < 64
    kind = (iota((384, 128), 1) % 64) // 8
    lift_r = jnp.where(kind == iota((384, 128), 0) // FACE + 1, dot3(lift[...], many, NT), 0.0)
    g = jnp.where(lane_n % 64 < 8, -dot3(mass[...], many, NT), 0.0)
    l_hi, l_lo = halves(lift_r[128:384])
    g = g + (dot1(pick[...], l_hi) + dot1(pick[...], l_lo))
    g = g + jnp.concatenate([lift_r[0:64], jnp.zeros((384, 128), F32), lift_r[64:128]], 0)
    g_hi, g_lo = halves(g)
    g_cat[...] = jnp.where(first_half, g_hi, g_lo)
    g_top[...] = jnp.where(first_half, g_hi, jnp.zeros_like(g_hi))
    rr = dot3(restrict[...], rhs[...], NT)
    weight = 1.0 + jnp.sum(onehot[...], 0, keepdims=True)
    weight = jnp.broadcast_to(weight, (8, 128))
    per = 1.0 / weight
    d_row = 1.0 / jnp.concatenate([coef[s // 4, s % 4 : s % 4 + 1, :] for s in range(16)], 1)

    low32 = lane < FACE
    nothing = jnp.zeros((32, 128), F32)
    for s in range(16):
        x, y = s // 4, s % 4
        rows = slice(32 * s, 32 * s + 32)
        above = first[32 * s + 128 : 32 * s + 160, 0:128] if x < 3 else nothing
        below = first[32 * s - 128 : 32 * s - 96, 384:512] if x > 0 else nothing
        faces[rows, 0:128] = jnp.where(low32, above, below)
        above = tr[32 * s + 32 : 32 * s + 64, 0:128] if y < 3 else nothing
        below = tr[32 * s - 32 : 32 * s, 0:128] if y > 0 else nothing
        faces[rows, 128:256] = jnp.where(low32, below, above)

    for copy in a_copies:
        copy.wait_recv()
    faces[0:64, 0:128] = jnp.where(low, faces[0:64, 0:128], swap(in_a[0]))
    faces[64:128, 0:128] = jnp.where(low, faces[64:128, 0:128], in_a[0])
    faces[384:448, 0:128] = jnp.where(low, in_a[1], faces[384:448, 0:128])
    faces[448:512, 0:128] = jnp.where(low, swap(in_a[1]), faces[448:512, 0:128])
    for i in range(4):
        half = slice(32 * (i % 2), 32 * (i % 2) + 32)
        below, above = in_a[2, half, :], in_a[3, half, :]
        below = below if i < 2 else swap(below)
        above = swap(above) if i < 2 else above
        j = 128 * i
        faces[j : j + 32, 128:256] = jnp.where(low32, below, faces[j : j + 32, 128:256])
        j = 128 * i + 96
        faces[j : j + 32, 128:256] = jnp.where(low32, faces[j : j + 32, 128:256], above)
    for s in range(16):
        own = tr[32 * s : 32 * s + 32, 128:256]
        below = jnp.where(row == 0, jnp.broadcast_to(in_z[0, s : s + 1, :], (32, 128)), pltpu.roll(own, 1, 0))
        above = jnp.where(row == 31, jnp.broadcast_to(in_z[1, s : s + 1, :], (32, 128)), pltpu.roll(own, 31, 0))
        faces[32 * s : 32 * s + 32, 256:384] = jnp.where(low32, below, above)

    v[...] = v[...] + dot3(faces[...], lift[...])
    u[...] = u[...] + dot3(v[...], smoother[...])
    s_hi, s_lo = halves(u[...])
    w = (dot1(s_hi, g_cat[...]) + dot1(s_lo, g_top[...])).T
    w = w[0:64] + w[64:128]
    c[...] = jnp.concatenate([w[0:8] + rr, w[8:64] * d_row], 0)

    b_copies = [
        shifted(0, 0, c.at[16:24, 384:512], in_bx.at[0], sb.at[0], rb.at[0]).start(),
        shifted(0, 1, c.at[8:16, 0:128], in_bx.at[1], sb.at[1], rb.at[1]).start(),
        shifted(1, 0, c.at[24:32, :], in_by.at[0], sb.at[2], rb.at[2]).start(),
        shifted(1, 1, c.at[32:40, :], in_by.at[1], sb.at[3], rb.at[3]).start(),
        shifted(2, 0, c.at[40:48, :], in_bz.at[0], sb.at[4], rb.at[4]).start(),
        shifted(2, 1, c.at[48:56, :], in_bz.at[1], sb.at[5], rb.at[5]).start(),
    ]
    first[...] = u[...] * d4(dcol[...])

    small = c[0:8, :]
    none8 = jnp.zeros((8, 128), F32)
    place = iota((8, N), 1)
    py, pz = (place // 32) % 4, place % 32
    small = small + jnp.concatenate([c[8:16, 128:512], none8], 1)
    small = small + jnp.concatenate([none8, c[16:24, 0:384]], 1)
    small = small + jnp.where(py > 0, pltpu.roll(c[24:32, :], 32, 1), 0.0)
    small = small + jnp.where(py < 3, pltpu.roll(c[32:40, :], N - 32, 1), 0.0)
    small = small + jnp.where(pz > 0, pltpu.roll(c[40:48, :], 1, 1), 0.0)
    small = small + jnp.where(pz < 31, pltpu.roll(c[48:56, :], N - 1, 1), 0.0)
    one = onehot[...].astype(BF16)
    r_hi, r_lo = halves(restrict[...])
    r_hi, r_lo = r_hi.astype(F32), r_lo.astype(F32)
    r_stack = jnp.concatenate([r_hi, r_hi, r_lo], 0).astype(BF16)

    for copy in b_copies:
        copy.wait_recv()
    zeros_mid = jnp.zeros((8, 256), F32)
    small = small + jnp.concatenate([in_bx[0], zeros_mid, in_bx[1]], 1)
    small = small + jnp.where(py == 0, pltpu.roll(in_by[0], N - 96, 1), 0.0)
    small = small + jnp.where(py == 3, pltpu.roll(in_by[1], 96, 1), 0.0)
    small = small + jnp.where(pz == 0, pltpu.roll(in_bz[0], N - 31, 1), 0.0)
    small = small + jnp.where(pz == 31, pltpu.roll(in_bz[1], 31, 1), 0.0)
    m_hi, m_lo = halves(small)
    parts = dot1(jnp.concatenate([m_hi.astype(F32), m_lo.astype(F32)], 0).astype(BF16), one)
    coarse_rhs = parts[0:8] + parts[8:16]
    zone = coarse_rhs * per
    zone_out[...] = zone

    z_copies = [
        Message(zone_out, in_zone.at[n], sz.at[n], rz.at[n], device, None, None).start()
        for n, device in enumerate(line)
    ]
    for dim in (1, 2):
        for way in (0, 1):
            n = ngx - 1 + 2 * (dim - 1) + way
            z_copies.append(shifted(dim, way, zone_out, in_zone.at[n], sz.at[n], rz.at[n]).start())

    two = zone + (coarse_rhs - (weight * dot3(cbm[...], zone) - zone)) * per

    for copy in z_copies:
        copy.wait_recv()
    total = in_zone[0]
    for n in range(1, ngx + 3):
        total = total + in_zone[n]
    two = two + total * per
    t_hi, t_lo = halves(two)
    t_hi, t_lo = t_hi.astype(F32), t_lo.astype(F32)
    t_stack = jnp.concatenate([t_hi, t_lo, t_hi], 0).astype(BF16)
    spread = lax.dot_general(t_stack, r_stack, TN, preferred_element_type=F32)
    e_hi, e_lo = halves(spread)
    spread = jnp.where(iota((128, N), 0) < 64, e_hi, e_lo)
    out_ref[...] = first[...] + dot1(one, spread)

    for copy in a_copies + b_copies + z_copies:
        copy.wait_send()


def shards(sizes, rhs, coef, mass, smoother, lift, restrict, coarse_block_matrix, element_cluster_index):
    others = sizes[0] - 1 + 4
    hbm = pl.BlockSpec(memory_space=pl.ANY)
    dma = pltpu.SemaphoreType.DMA
    out = pl.pallas_call(
        functools.partial(kernel, sizes),
        out_shape=jax.ShapeDtypeStruct((N, N), F32),
        in_specs=[hbm] * 8,
        out_specs=pl.BlockSpec(memory_space=pltpu.VMEM),
        scratch_shapes=[
            pltpu.VMEM((N, N), F32),
            pltpu.VMEM((N, N), F32),
            pltpu.VMEM((N, N), F32),
            pltpu.VMEM((384, N), F32),
            pltpu.VMEM((8, N), F32),
            pltpu.VMEM((8, 8), F32),
            pltpu.VMEM((4, 4, 32), F32),
            pltpu.VMEM((4, 4, 32), jnp.int32),
            pltpu.VMEM((N, 128), F32),
            pltpu.VMEM((N, 128), F32),
            pltpu.VMEM((N, 256), BF16),
            pltpu.VMEM((N, N), F32),
            pltpu.VMEM((N, N), F32),
            pltpu.VMEM((N, 256), F32),
            pltpu.VMEM((N, 384), F32),
            pltpu.VMEM((N, N), F32),
            pltpu.VMEM((N, 128), BF16),
            pltpu.VMEM((N, 128), BF16),
            pltpu.VMEM((4, FACE, 128), F32),
            pltpu.VMEM((4, FACE, 128), F32),
            pltpu.VMEM((2, 16, 128), F32),
            pltpu.VMEM((2, 16, 128), F32),
            pltpu.VMEM((FACE, N), F32),
            pltpu.VMEM((2, 8, 128), F32),
            pltpu.VMEM((2, 8, N), F32),
            pltpu.VMEM((2, 8, N), F32),
            pltpu.VMEM((8, 128), F32),
            pltpu.VMEM((others, 8, 128), F32),
            dma((10,)),
            dma((6,)),
            dma((6,)),
            dma((6,)),
            dma((6,)),
            dma((others,)),
            dma((others,)),
        ],
        compiler_params=pltpu.CompilerParams(
            collective_id=0, has_side_effects=True, vmem_limit_bytes=62 * 1024 * 1024
        ),
        name="cycle",
    )(rhs.reshape(N, N), coef, mass, smoother, lift, restrict.T, coarse_block_matrix, element_cluster_index)
    return out.reshape(rhs.shape)


def solution(mesh):
    sizes = tuple(mesh.shape[a] for a in ("gx", "gy", "gz"))
    return jax.shard_map(
        functools.partial(shards, sizes),
        mesh=mesh,
        in_specs=(
            P("gx", "gy", "gz", None),
            P("gx", "gy", "gz"),
            P(),
            P(),
            P(),
            P(),
            P(),
            P("gx", "gy", "gz"),
        ),
        out_specs=P("gx", "gy", "gz", None),
        check_vma=False,
    )
```

time: 49.8 us -> 36.4 us (0.73)
  the two profiles are of different devices: /device:TPU:1 before, /device:TPU:57 now
where the time goes in v2:
time: 36.4 us; the launch traced here: 36.3 us
  Pallas kernels  34 us (93%)
  local copies, waits for them, and re-layouts  2.29 us (6%)
    pallas_call x1, Pallas kernels, shards(): pl.pallas_call(functools.partial(kernel, sizes), out_shape=jax.ShapeDtype...  34 us
    unnamed x1, local copies, waits for them, and re-layouts  2.29 us

profile of v2, /device:TPU:57, one launch (start us, length us, event | category | flops | bytes accessed | tf_op | source)
XLA Modules:
  0.0 36.3 jit_solution(4173799300129722559)
XLA Ops:
  0.0 34.0 %cycle.1 = f32[512,512]{1,0:T(8,128)} custom-call(f32[512,512]{1,0:T(8,128)} %bitcast.4, f32[4,4,32]{2,1,0:T(4,128)} %coef_hbm.1, f32[512,512]{1,0:T(8,128)} %mass_hbm.1, f32[512,512]{1,0:T(8,128)} %smoother_hbm.1, f32[384,512]{1,0:T(8,128)} %lift_hbm.1, f32[8,512]{1,0:T(8,128)} %bitcast.5, f32[8,8]{1,0:T(8,128)} %cbm_hbm.1, s32[4,4,32]{2,1,0:T(4,128)} %label_hbm.1), custom_call_target="tpu_custom_call" | custom-call | tf_op jit(solution)/shard_map/cycle/pallas_call | solution.py:325
  34.0 2.3 %copy.10 = f32[4,4,32,512]{3,2,1,0:T(8,128)} copy(f32[4,4,32,512]{3,2,1,0:T(8,128)} %bitcast.3) | data formatting | bytes 2097152

commit v3 on v2

--- a/solution.py
+++ b/solution.py
@@ -38,7 +38,7 @@
     sizes, rhs_hbm, coef_hbm, mass_hbm, smoother_hbm, lift_hbm, restrict_hbm, cbm_hbm, label_hbm,
     out_ref,
     rhs, mass, smoother, lift, restrict, cbm, coef, label,
-    dcol, onehot, pick, u, first, tr, faces, v, g_cat, g_top,
+    dcol, onehot, pick, u, first, tr, faces, v, g_cat, g_top, lz, lzg, wide, rows_z,
     out_a, in_a, out_z, in_z, c, in_bx, in_by, in_bz, zone_out, in_zone,
     load_sem, sa, ra, sb, rb, sz, rz,
 ):
@@ -159,12 +159,25 @@
     u[...] = dot3(rhs[...], smoother[...])
     first[...] = u[...] * d4(dcol[...])
 
+    for s in range(16):
+        rows_z[s : s + 1, :] = first[32 * s + 31 : 32 * s + 32, :]
+        rows_z[16 + s : 17 + s, :] = first[32 * s : 32 * s + 1, :]
+    ends = rows_z[...]
+    e_hi, e_lo = halves(ends)
+    ends = dot1(e_hi, pick[:, 128:256]) + dot1(e_lo, pick[:, 128:256])
+    out_z[0] = ends[0:16]
+    out_z[1] = ends[16:32]
+    pl.semaphore_wait(barrier, partners)
+    z_traces = [
+        shifted(2, way, out_z.at[way], in_z.at[way], sa.at[4 + way], ra.at[4 + way]).start()
+        for way in (0, 1)
+    ]
+
     low = iota((FACE, 128), 1) < FACE
     swap = lambda a: pltpu.roll(a, FACE, 1)
     top, bottom = first[384:512, 384:512], first[0:128, 0:128]
     out_a[0] = jnp.where(low, swap(top[0:64]), top[64:128])
     out_a[1] = jnp.where(low, bottom[0:64], swap(bottom[64:128]))
-    pl.semaphore_wait(barrier, partners)
     a_copies = [
         shifted(0, way, out_a.at[way], in_a.at[way], sa.at[way], ra.at[way]).start() for way in (0, 1)
     ]
@@ -175,18 +188,10 @@
     ybottom = [tr[128 * i : 128 * i + 32, 0:128] for i in range(4)]
     out_a[2] = jnp.where(low, jnp.concatenate(ytop[:2], 0), swap(jnp.concatenate(ytop[2:], 0)))
     out_a[3] = jnp.where(low, swap(jnp.concatenate(ybottom[:2], 0)), jnp.concatenate(ybottom[2:], 0))
-    for s in range(16):
-        out_z[0, s : s + 1, :] = tr[32 * s + 31 : 32 * s + 32, 128:256]
-        out_z[1, s : s + 1, :] = tr[32 * s : 32 * s + 1, 128:256]
     a_copies += [
         shifted(1, way, out_a.at[2 + way], in_a.at[2 + way], sa.at[2 + way], ra.at[2 + way]).start()
         for way in (0, 1)
     ]
-    a_copies += [
-        shifted(2, way, out_z.at[way], in_z.at[way], sa.at[4 + way], ra.at[4 + way]).start()
-        for way in (0, 1)
-    ]
-
     for copy in loads[4:]:
         copy.wait()
 
@@ -205,6 +210,9 @@
     g_cat[...] = jnp.where(first_half, g_hi, g_lo)
     g_top[...] = jnp.where(first_half, g_hi, jnp.zeros_like(g_hi))
     rr = dot3(restrict[...], rhs[...], NT)
+    lz[...] = dot3(lift[256:384, :], smoother[...])
+    lz_hi, lz_lo = halves(lz[...])
+    lzg[...] = dot1(lz_hi, g_cat[...]) + dot1(lz_lo, g_top[...])
     weight = 1.0 + jnp.sum(onehot[...], 0, keepdims=True)
     weight = jnp.broadcast_to(weight, (8, 128))
     per = 1.0 / weight
@@ -221,6 +229,10 @@
         above = tr[32 * s + 32 : 32 * s + 64, 0:128] if y < 3 else nothing
         below = tr[32 * s - 32 : 32 * s, 0:128] if y > 0 else nothing
         faces[rows, 128:256] = jnp.where(low32, below, above)
+        own = tr[rows, 128:256]
+        below = jnp.where(row == 0, 0.0, pltpu.roll(own, 1, 0))
+        above = jnp.where(row == 31, 0.0, pltpu.roll(own, 31, 0))
+        faces[rows, 256:384] = jnp.where(low32, below, above)
 
     for copy in a_copies:
         copy.wait_recv()
@@ -237,27 +249,36 @@
         faces[j : j + 32, 128:256] = jnp.where(low32, below, faces[j : j + 32, 128:256])
         j = 128 * i + 96
         faces[j : j + 32, 128:256] = jnp.where(low32, faces[j : j + 32, 128:256], above)
-    for s in range(16):
-        own = tr[32 * s : 32 * s + 32, 128:256]
-        below = jnp.where(row == 0, jnp.broadcast_to(in_z[0, s : s + 1, :], (32, 128)), pltpu.roll(own, 1, 0))
-        above = jnp.where(row == 31, jnp.broadcast_to(in_z[1, s : s + 1, :], (32, 128)), pltpu.roll(own, 31, 0))
-        faces[32 * s : 32 * s + 32, 256:384] = jnp.where(low32, below, above)
 
     v[...] = v[...] + dot3(faces[...], lift[...])
     u[...] = u[...] + dot3(v[...], smoother[...])
     s_hi, s_lo = halves(u[...])
-    w = (dot1(s_hi, g_cat[...]) + dot1(s_lo, g_top[...])).T
+    wide[...] = dot1(s_hi, g_cat[...]) + dot1(s_lo, g_top[...])
+
+    for copy in z_traces:
+        copy.wait_recv()
+    low16 = iota((16, 128), 1) < FACE
+    ends = jnp.concatenate([jnp.where(low16, in_z[0], 0.0), jnp.where(low16, 0.0, in_z[1])], 0)
+    more = dot3(ends, lzg[...])
+    wide[pl.ds(0, 16, stride=32), :] = wide[pl.ds(0, 16, stride=32), :] + more[0:16]
+    wide[pl.ds(31, 16, stride=32), :] = wide[pl.ds(31, 16, stride=32), :] + more[16:32]
+    w = wide[...].T
     w = w[0:64] + w[64:128]
     c[...] = jnp.concatenate([w[0:8] + rr, w[8:64] * d_row], 0)
 
     b_copies = [
+        shifted(2, 0, c.at[40:48, :], in_bz.at[0], sb.at[4], rb.at[4]).start(),
+        shifted(2, 1, c.at[48:56, :], in_bz.at[1], sb.at[5], rb.at[5]).start(),
         shifted(0, 0, c.at[16:24, 384:512], in_bx.at[0], sb.at[0], rb.at[0]).start(),
         shifted(0, 1, c.at[8:16, 0:128], in_bx.at[1], sb.at[1], rb.at[1]).start(),
         shifted(1, 0, c.at[24:32, :], in_by.at[0], sb.at[2], rb.at[2]).start(),
         shifted(1, 1, c.at[32:40, :], in_by.at[1], sb.at[3], rb.at[3]).start(),
-        shifted(2, 0, c.at[40:48, :], in_bz.at[0], sb.at[4], rb.at[4]).start(),
-        shifted(2, 1, c.at[48:56, :], in_bz.at[1], sb.at[5], rb.at[5]).start(),
-    ]
+    ]
+    more = dot3(ends, lz[...])
+    for start, part in ((0, more[0:16]), (31, more[16:32])):
+        for s in range(16):
+            at = 32 * s + start
+            u[at : at + 1, :] = u[at : at + 1, :] + part[s : s + 1]
     first[...] = u[...] * d4(dcol[...])
 
     small = c[0:8, :]
@@ -289,14 +310,15 @@
     zone = coarse_rhs * per
     zone_out[...] = zone
 
-    z_copies = [
-        Message(zone_out, in_zone.at[n], sz.at[n], rz.at[n], device, None, None).start()
-        for n, device in enumerate(line)
-    ]
-    for dim in (1, 2):
+    z_copies = []
+    for dim in (2, 1):
         for way in (0, 1):
             n = ngx - 1 + 2 * (dim - 1) + way
             z_copies.append(shifted(dim, way, zone_out, in_zone.at[n], sz.at[n], rz.at[n]).start())
+    z_copies += [
+        Message(zone_out, in_zone.at[n], sz.at[n], rz.at[n], device, None, None).start()
+        for n, device in enumerate(line)
+    ]
 
     two = zone + (coarse_rhs - (weight * dot3(cbm[...], zone) - zone)) * per
 
@@ -314,7 +336,7 @@
     spread = jnp.where(iota((128, N), 0) < 64, e_hi, e_lo)
     out_ref[...] = first[...] + dot1(one, spread)
 
-    for copy in a_copies + b_copies + z_copies:
+    for copy in z_traces + a_copies + b_copies + z_copies:
         copy.wait_send()
 
 
@@ -324,7 +346,7 @@
     dma = pltpu.SemaphoreType.DMA
     out = pl.pallas_call(
         functools.partial(kernel, sizes),
-        out_shape=jax.ShapeDtypeStruct((N, N), F32),
+        out_shape=pltpu.VMEM((N, N), F32),
         in_specs=[hbm] * 8,
         out_specs=pl.BlockSpec(memory_space=pltpu.VMEM),
         scratch_shapes=[
@@ -346,6 +368,10 @@
             pltpu.VMEM((N, N), F32),
             pltpu.VMEM((N, 128), BF16),
             pltpu.VMEM((N, 128), BF16),
+            pltpu.VMEM((128, N), F32),
+            pltpu.VMEM((128, 128), F32),
+            pltpu.VMEM((N, 128), F32),
+            pltpu.VMEM((32, N), F32),
             pltpu.VMEM((4, FACE, 128), F32),
             pltpu.VMEM((4, FACE, 128), F32),
             pltpu.VMEM((2, 16, 128), F32),
@@ -365,10 +391,13 @@
             dma((others,)),
         ],
         compiler_params=pltpu.CompilerParams(
-            collective_id=0, has_side_effects=True, vmem_limit_bytes=62 * 1024 * 1024
+            collective_id=0, has_side_effects=True, vmem_limit_bytes=40 * 1024 * 1024
         ),
         name="cycle",
-    )(rhs.reshape(N, N), coef, mass, smoother, lift, restrict.T, coarse_block_matrix, element_cluster_index)
+    )(*[
+        pltpu.with_memory_space_constraint(a, pltpu.HBM)
+        for a in (rhs.reshape(N, N), coef, mass, smoother, lift, restrict.T, coarse_block_matrix, element_cluster_index)
+    ])
     return out.reshape(rhs.shape)
 
 

time: 36.4 us -> 31.7 us (0.87)
  the two profiles are of different devices: /device:TPU:57 before, /device:TPU:1 now
where the time goes in v3:
time: 31.7 us; the launch traced here: 31.5 us
  Pallas kernels  30.5 us (96%)
  local copies, waits for them, and re-layouts  0.97 us (3%)
    pallas_call x1, Pallas kernels, shards(): pl.pallas_call(functools.partial(kernel, sizes), out_shape=pltpu.VMEM((N,...  30.5 us
    unnamed x1, local copies, waits for them, and re-layouts  0.97 us

profile of v3, /device:TPU:1, one launch (start us, length us, event | category | flops | bytes accessed | tf_op | source)
XLA Modules:
  0.0 31.5 jit_solution(9668499966803936398)
XLA Ops:
  0.0 30.5 %cycle.1 = f32[512,512]{1,0:T(8,128)S(1)} custom-call(f32[512,512]{1,0:T(8,128)} %bitcast.4, f32[4,4,32]{2,1,0:T(4,128)} %coef_hbm.1, f32[512,512]{1,0:T(8,128)} %mass_hbm.1, f32[512,512]{1,0:T(8,128)} %smoother_hbm.1, f32[384,512]{1,0:T(8,128)} %lift_hbm.1, f32[8,512]{1,0:T(8,128)} %bitcast.5, f32[8,8]{1,0:T(8,128)} %cbm_hbm.1, s32[4,4,32]{2,1,0:T(4,128)} %label_hbm.1), custom_call_target="tpu_custom_call" | custom-call | tf_op jit(solution)/shard_map/cycle/pallas_call | solution.py:347
  30.6 1.0 %copy.10 = f32[4,4,32,512]{3,2,1,0:T(8,128)} copy(f32[4,4,32,512]{3,2,1,0:T(8,128)S(1)} %bitcast.3) | data formatting | bytes 2097152

commit v4 on v3

--- a/solution.py
+++ b/solution.py
@@ -38,8 +38,8 @@
     sizes, rhs_hbm, coef_hbm, mass_hbm, smoother_hbm, lift_hbm, restrict_hbm, cbm_hbm, label_hbm,
     out_ref,
     rhs, mass, smoother, lift, restrict, cbm, coef, label,
-    dcol, onehot, pick, u, first, tr, faces, v, g_cat, g_top, lz, lzg, wide, rows_z,
-    out_a, in_a, out_z, in_z, c, in_bx, in_by, in_bz, zone_out, in_zone,
+    dcol, onehot, pick, u, first, tr, faces, v, lsg, wide, rows_z,
+    out_a, in_a, out_z, in_z, c, c_z, in_bx, in_by, in_bz, zone_out, in_zone,
     load_sem, sa, ra, sb, rb, sz, rz,
 ):
     ngx, ngy, ngz = sizes
@@ -62,7 +62,7 @@
             ]
         )
     ]
-    for copy in loads:
+    for copy in loads[:6]:
         copy.start()
 
     def along(dim, step):
@@ -126,7 +126,7 @@
                 elif dim == 1:
                     in_by[way] = jnp.zeros((8, N), F32)
                 else:
-                    in_bz[way] = jnp.zeros((8, N), F32)
+                    in_bz[way] = jnp.zeros((16, N), F32)
                 if dim > 0:
                     in_zone[ngx - 1 + 2 * (dim - 1) + way] = jnp.zeros((8, 128), F32)
 
@@ -156,6 +156,8 @@
 
     loads[2].wait()
     loads[3].wait()
+    for copy in loads[6:]:
+        copy.start()
     u[...] = dot3(rhs[...], smoother[...])
     first[...] = u[...] * d4(dcol[...])
 
@@ -195,24 +197,34 @@
     for copy in loads[4:]:
         copy.wait()
 
-    v[...] = rhs[...] - dot3(u[...], mass[...])
-
-    many = jnp.concatenate([restrict[...]] * 16, 0)
     lane_n = iota((N, 128), 1)
     first_half = lane_n < 64
+
+    def table(a):
+        hi, lo = halves(a)
+        top = first_half[0 : a.shape[0]]
+        return jnp.where(top, hi, lo), jnp.where(top, hi, jnp.zeros_like(hi))
+
+    def project(a, columns):
+        hi, lo = halves(a)
+        t = dot1(hi, columns[0]) + dot1(lo, columns[1])
+        return t + swap(t)
+
+    many = jnp.concatenate([restrict[...]] * 16, 0)
+    block = iota((384, 128), 0) // FACE
     kind = (iota((384, 128), 1) % 64) // 8
-    lift_r = jnp.where(kind == iota((384, 128), 0) // FACE + 1, dot3(lift[...], many, NT), 0.0)
+    lift_r = jnp.where(kind == jnp.where(block < 5, block + 1, 7), dot3(lift[...], many, NT), 0.0)
     g = jnp.where(lane_n % 64 < 8, -dot3(mass[...], many, NT), 0.0)
     l_hi, l_lo = halves(lift_r[128:384])
     g = g + (dot1(pick[...], l_hi) + dot1(pick[...], l_lo))
     g = g + jnp.concatenate([lift_r[0:64], jnp.zeros((384, 128), F32), lift_r[64:128]], 0)
-    g_hi, g_lo = halves(g)
-    g_cat[...] = jnp.where(first_half, g_hi, g_lo)
-    g_top[...] = jnp.where(first_half, g_hi, jnp.zeros_like(g_hi))
-    rr = dot3(restrict[...], rhs[...], NT)
-    lz[...] = dot3(lift[256:384, :], smoother[...])
-    lz_hi, lz_lo = halves(lz[...])
-    lzg[...] = dot1(lz_hi, g_cat[...]) + dot1(lz_lo, g_top[...])
+    sg = project(smoother[...], table(g))
+    sg_table = table(sg)
+    lsg[...] = project(lift[...], sg_table)
+    l_table = table(lsg[...])
+    msg = project(mass[...], sg_table)
+    own = jnp.where(lane_n % 64 < 8, many.T, 0.0)
+    wide[...] = project(rhs[...], table(sg + own)) + project(u[...], table(g - msg))
     weight = 1.0 + jnp.sum(onehot[...], 0, keepdims=True)
     weight = jnp.broadcast_to(weight, (8, 128))
     per = 1.0 / weight
@@ -250,36 +262,49 @@
         j = 128 * i + 96
         faces[j : j + 32, 128:256] = jnp.where(low32, faces[j : j + 32, 128:256], above)
 
-    v[...] = v[...] + dot3(faces[...], lift[...])
-    u[...] = u[...] + dot3(v[...], smoother[...])
-    s_hi, s_lo = halves(u[...])
-    wide[...] = dot1(s_hi, g_cat[...]) + dot1(s_lo, g_top[...])
+    wide[...] = wide[...] + project(faces[...], l_table)
+    w = wide[...].T
+    c_z[...] = jnp.concatenate([w[40:48] * d_row, jnp.broadcast_to(d_row, (8, N)), w[56:64] * d_row], 0)
+    z_ways = [
+        shifted(2, 0, c_z.at[0:16, :], in_bz.at[0], sb.at[4], rb.at[4]).start(),
+        shifted(2, 1, c_z.at[8:24, :], in_bz.at[1], sb.at[5], rb.at[5]).start(),
+    ]
 
     for copy in z_traces:
         copy.wait_recv()
     low16 = iota((16, 128), 1) < FACE
-    ends = jnp.concatenate([jnp.where(low16, in_z[0], 0.0), jnp.where(low16, 0.0, in_z[1])], 0)
-    more = dot3(ends, lzg[...])
-    wide[pl.ds(0, 16, stride=32), :] = wide[pl.ds(0, 16, stride=32), :] + more[0:16]
-    wide[pl.ds(31, 16, stride=32), :] = wide[pl.ds(31, 16, stride=32), :] + more[16:32]
+    ends = jnp.concatenate(
+        [
+            jnp.where(low16, in_z[0], 0.0),
+            jnp.where(low16, 0.0, in_z[1]),
+            jnp.where(low16, out_z[0], 0.0),
+            jnp.where(low16, 0.0, out_z[1]),
+        ],
+        0,
+    )
+    more = dot3(ends, lsg[256:384, :])
+    lane16 = iota((16, 128), 1)
+    back = (lane16 >= 48) & (lane16 < 56)
+    low_rows = more[0:16] + jnp.where(back, pltpu.roll(more[48:64], 8, 1), 0.0)
+    high_rows = more[16:32] + jnp.where(back, pltpu.roll(more[32:48], 120, 1), 0.0)
+    wide[pl.ds(0, 16, stride=32), :] = wide[pl.ds(0, 16, stride=32), :] + low_rows
+    wide[pl.ds(31, 16, stride=32), :] = wide[pl.ds(31, 16, stride=32), :] + high_rows
     w = wide[...].T
-    w = w[0:64] + w[64:128]
-    c[...] = jnp.concatenate([w[0:8] + rr, w[8:64] * d_row], 0)
+    c[...] = jnp.concatenate([w[0:8], w[8:48] * d_row, w[48:56], w[56:64] * d_row], 0)
 
     b_copies = [
-        shifted(2, 0, c.at[40:48, :], in_bz.at[0], sb.at[4], rb.at[4]).start(),
-        shifted(2, 1, c.at[48:56, :], in_bz.at[1], sb.at[5], rb.at[5]).start(),
         shifted(0, 0, c.at[16:24, 384:512], in_bx.at[0], sb.at[0], rb.at[0]).start(),
         shifted(0, 1, c.at[8:16, 0:128], in_bx.at[1], sb.at[1], rb.at[1]).start(),
         shifted(1, 0, c.at[24:32, :], in_by.at[0], sb.at[2], rb.at[2]).start(),
         shifted(1, 1, c.at[32:40, :], in_by.at[1], sb.at[3], rb.at[3]).start(),
-    ]
-    more = dot3(ends, lz[...])
-    for start, part in ((0, more[0:16]), (31, more[16:32])):
-        for s in range(16):
-            at = 32 * s + start
-            u[at : at + 1, :] = u[at : at + 1, :] + part[s : s + 1]
-    first[...] = u[...] * d4(dcol[...])
+    ] + z_ways
+
+    for s in range(16):
+        at = 32 * s
+        faces[at : at + 1, 256:384] = jnp.where(lane[0:1] < FACE, in_z[0, s : s + 1, :], faces[at : at + 1, 256:384])
+        at = 32 * s + 31
+        faces[at : at + 1, 256:384] = jnp.where(lane[0:1] < FACE, faces[at : at + 1, 256:384], in_z[1, s : s + 1, :])
+    v[...] = rhs[...] - dot3(u[...], mass[...])
 
     small = c[0:8, :]
     none8 = jnp.zeros((8, 128), F32)
@@ -290,7 +315,7 @@
     small = small + jnp.where(py > 0, pltpu.roll(c[24:32, :], 32, 1), 0.0)
     small = small + jnp.where(py < 3, pltpu.roll(c[32:40, :], N - 32, 1), 0.0)
     small = small + jnp.where(pz > 0, pltpu.roll(c[40:48, :], 1, 1), 0.0)
-    small = small + jnp.where(pz < 31, pltpu.roll(c[48:56, :], N - 1, 1), 0.0)
+    small = small + jnp.where(pz < 31, pltpu.roll(c[56:64, :], N - 1, 1), 0.0)
     one = onehot[...].astype(BF16)
     r_hi, r_lo = halves(restrict[...])
     r_hi, r_lo = r_hi.astype(F32), r_lo.astype(F32)
@@ -302,8 +327,9 @@
     small = small + jnp.concatenate([in_bx[0], zeros_mid, in_bx[1]], 1)
     small = small + jnp.where(py == 0, pltpu.roll(in_by[0], N - 96, 1), 0.0)
     small = small + jnp.where(py == 3, pltpu.roll(in_by[1], 96, 1), 0.0)
-    small = small + jnp.where(pz == 0, pltpu.roll(in_bz[0], N - 31, 1), 0.0)
-    small = small + jnp.where(pz == 31, pltpu.roll(in_bz[1], 31, 1), 0.0)
+    z_low, z_high = pltpu.roll(in_bz[0], N - 31, 1), pltpu.roll(in_bz[1], 31, 1)
+    small = small + jnp.where(pz == 0, z_low[0:8] + z_low[8:16] * c[48:56, :], 0.0)
+    small = small + jnp.where(pz == 31, z_high[8:16] + z_high[0:8] * c[48:56, :], 0.0)
     m_hi, m_lo = halves(small)
     parts = dot1(jnp.concatenate([m_hi.astype(F32), m_lo.astype(F32)], 0).astype(BF16), one)
     coarse_rhs = parts[0:8] + parts[8:16]
@@ -320,6 +346,8 @@
         for n, device in enumerate(line)
     ]
 
+    v[...] = v[...] + dot3(faces[...], lift[...])
+    first[...] = (u[...] + dot3(v[...], smoother[...])) * d4(dcol[...])
     two = zone + (coarse_rhs - (weight * dot3(cbm[...], zone) - zone)) * per
 
     for copy in z_copies:
@@ -366,10 +394,7 @@
             pltpu.VMEM((N, 256), F32),
             pltpu.VMEM((N, 384), F32),
             pltpu.VMEM((N, N), F32),
-            pltpu.VMEM((N, 128), BF16),
-            pltpu.VMEM((N, 128), BF16),
-            pltpu.VMEM((128, N), F32),
-            pltpu.VMEM((128, 128), F32),
+            pltpu.VMEM((384, 128), F32),
             pltpu.VMEM((N, 128), F32),
             pltpu.VMEM((32, N), F32),
             pltpu.VMEM((4, FACE, 128), F32),
@@ -377,9 +402,10 @@
             pltpu.VMEM((2, 16, 128), F32),
             pltpu.VMEM((2, 16, 128), F32),
             pltpu.VMEM((FACE, N), F32),
+            pltpu.VMEM((24, N), F32),
             pltpu.VMEM((2, 8, 128), F32),
             pltpu.VMEM((2, 8, N), F32),
-            pltpu.VMEM((2, 8, N), F32),
+            pltpu.VMEM((2, 16, N), F32),
             pltpu.VMEM((8, 128), F32),
             pltpu.VMEM((others, 8, 128), F32),
             dma((10,)),

time: 31.7 us -> 30 us (0.946)
  Pallas kernels: 30.5 us -> 28.8 us
    pallas_call x1, Pallas kernels: 30.5 us -> 28.8 us  [shards(): pl.pallas_call(functools.partial(kernel, sizes), out_shape=pltpu.VMEM((N,...]
where the time goes in v4:
time: 30 us; the launch traced here: 29.8 us
  Pallas kernels  28.8 us (96%)
  local copies, waits for them, and re-layouts  0.97 us (3%)
    pallas_call x1, Pallas kernels, shards(): pl.pallas_call(functools.partial(kernel, sizes), out_shape=pltpu.VMEM((N,...  28.8 us
    unnamed x1, local copies, waits for them, and re-layouts  0.97 us

profile of v4, /device:TPU:1, one launch (start us, length us, event | category | flops | bytes accessed | tf_op | source)
XLA Modules:
  0.0 29.8 jit_solution(16853044282594353980)
XLA Ops:
  0.0 28.8 %cycle.1 = f32[512,512]{1,0:T(8,128)S(1)} custom-call(f32[512,512]{1,0:T(8,128)} %bitcast.4, f32[4,4,32]{2,1,0:T(4,128)} %coef_hbm.1, f32[512,512]{1,0:T(8,128)} %mass_hbm.1, f32[512,512]{1,0:T(8,128)} %smoother_hbm.1, f32[384,512]{1,0:T(8,128)} %lift_hbm.1, f32[8,512]{1,0:T(8,128)} %bitcast.5, f32[8,8]{1,0:T(8,128)} %cbm_hbm.1, s32[4,4,32]{2,1,0:T(4,128)} %label_hbm.1), custom_call_target="tpu_custom_call" | custom-call | tf_op jit(solution)/shard_map/cycle/pallas_call | solution.py:375
  28.8 1.0 %copy.10 = f32[4,4,32,512]{3,2,1,0:T(8,128)} copy(f32[4,4,32,512]{3,2,1,0:T(8,128)S(1)} %bitcast.3) | data formatting | bytes 2097152

commit v5 on v4

--- a/solution.py
+++ b/solution.py
@@ -39,7 +39,7 @@
     out_ref,
     rhs, mass, smoother, lift, restrict, cbm, coef, label,
     dcol, onehot, pick, u, first, tr, faces, v, lsg, wide, rows_z,
-    out_a, in_a, out_z, in_z, c, c_z, in_bx, in_by, in_bz, zone_out, in_zone,
+    out_a, in_a, out_z, in_z, c, out_by, out_bz, in_bx, in_by, in_bz, zone_out, in_zone,
     load_sem, sa, ra, sb, rb, sz, rz,
 ):
     ngx, ngy, ngz = sizes
@@ -62,7 +62,7 @@
             ]
         )
     ]
-    for copy in loads[:6]:
+    for copy in loads:
         copy.start()
 
     def along(dim, step):
@@ -124,9 +124,9 @@
                 if dim == 0:
                     in_bx[way] = jnp.zeros((8, 128), F32)
                 elif dim == 1:
-                    in_by[way] = jnp.zeros((8, N), F32)
+                    in_by[way] = jnp.zeros((8, 128), F32)
                 else:
-                    in_bz[way] = jnp.zeros((16, N), F32)
+                    in_bz[way] = jnp.zeros((16, 128), F32)
                 if dim > 0:
                     in_zone[ngx - 1 + 2 * (dim - 1) + way] = jnp.zeros((8, 128), F32)
 
@@ -156,8 +156,6 @@
 
     loads[2].wait()
     loads[3].wait()
-    for copy in loads[6:]:
-        copy.start()
     u[...] = dot3(rhs[...], smoother[...])
     first[...] = u[...] * d4(dcol[...])
 
@@ -213,8 +211,10 @@
     many = jnp.concatenate([restrict[...]] * 16, 0)
     block = iota((384, 128), 0) // FACE
     kind = (iota((384, 128), 1) % 64) // 8
-    lift_r = jnp.where(kind == jnp.where(block < 5, block + 1, 7), dot3(lift[...], many, NT), 0.0)
-    g = jnp.where(lane_n % 64 < 8, -dot3(mass[...], many, NT), 0.0)
+    r_wide = many.T
+    r_table = table(r_wide)
+    lift_r = jnp.where(kind == jnp.where(block < 5, block + 1, 7), project(lift[...], r_table), 0.0)
+    g = jnp.where(lane_n % 64 < 8, -project(mass[...], r_table), 0.0)
     l_hi, l_lo = halves(lift_r[128:384])
     g = g + (dot1(pick[...], l_hi) + dot1(pick[...], l_lo))
     g = g + jnp.concatenate([lift_r[0:64], jnp.zeros((384, 128), F32), lift_r[64:128]], 0)
@@ -223,7 +223,7 @@
     lsg[...] = project(lift[...], sg_table)
     l_table = table(lsg[...])
     msg = project(mass[...], sg_table)
-    own = jnp.where(lane_n % 64 < 8, many.T, 0.0)
+    own = jnp.where(lane_n % 64 < 8, r_wide, 0.0)
     wide[...] = project(rhs[...], table(sg + own)) + project(u[...], table(g - msg))
     weight = 1.0 + jnp.sum(onehot[...], 0, keepdims=True)
     weight = jnp.broadcast_to(weight, (8, 128))
@@ -263,11 +263,12 @@
         faces[j : j + 32, 128:256] = jnp.where(low32, faces[j : j + 32, 128:256], above)
 
     wide[...] = wide[...] + project(faces[...], l_table)
-    w = wide[...].T
-    c_z[...] = jnp.concatenate([w[40:48] * d_row, jnp.broadcast_to(d_row, (8, N)), w[56:64] * d_row], 0)
+    lane16 = iota((16, 128), 1)
+    for way, at in ((0, 31), (1, 0)):
+        d_ends = dcol[pl.ds(at, 16, stride=32), :]
+        out_bz[way] = jnp.where(lane16 // 8 == 6, d_ends, d_ends * wide[pl.ds(at, 16, stride=32), :])
     z_ways = [
-        shifted(2, 0, c_z.at[0:16, :], in_bz.at[0], sb.at[4], rb.at[4]).start(),
-        shifted(2, 1, c_z.at[8:24, :], in_bz.at[1], sb.at[5], rb.at[5]).start(),
+        shifted(2, way, out_bz.at[way], in_bz.at[way], sb.at[4 + way], rb.at[4 + way]).start() for way in (0, 1)
     ]
 
     for copy in z_traces:
@@ -283,20 +284,26 @@
         0,
     )
     more = dot3(ends, lsg[256:384, :])
-    lane16 = iota((16, 128), 1)
-    back = (lane16 >= 48) & (lane16 < 56)
-    low_rows = more[0:16] + jnp.where(back, pltpu.roll(more[48:64], 8, 1), 0.0)
-    high_rows = more[16:32] + jnp.where(back, pltpu.roll(more[32:48], 120, 1), 0.0)
-    wide[pl.ds(0, 16, stride=32), :] = wide[pl.ds(0, 16, stride=32), :] + low_rows
-    wide[pl.ds(31, 16, stride=32), :] = wide[pl.ds(31, 16, stride=32), :] + high_rows
+    wide[pl.ds(0, 16, stride=32), :] = wide[pl.ds(0, 16, stride=32), :] + more[0:16]
+    wide[pl.ds(31, 16, stride=32), :] = wide[pl.ds(31, 16, stride=32), :] + more[16:32]
     w = wide[...].T
-    c[...] = jnp.concatenate([w[0:8], w[8:48] * d_row, w[48:56], w[56:64] * d_row], 0)
+    c[...] = jnp.concatenate([w[0:8], w[8:64] * d_row], 0)
+    quarter = iota((8, 128), 1) // 32
+
+    def gather_y(tiles, turns):
+        packed = jnp.zeros((8, 128), F32)
+        for i in range(4):
+            packed = jnp.where(quarter == i, pltpu.roll(tiles[i], turns[i], 1), packed)
+        return packed
+
+    out_by[0] = gather_y([c[24:32, 128 * i : 128 * i + 128] for i in range(4)], [32, 64, 96, 0])
+    out_by[1] = gather_y([c[32:40, 128 * i : 128 * i + 128] for i in range(4)], [0, 32, 64, 96])
 
     b_copies = [
         shifted(0, 0, c.at[16:24, 384:512], in_bx.at[0], sb.at[0], rb.at[0]).start(),
         shifted(0, 1, c.at[8:16, 0:128], in_bx.at[1], sb.at[1], rb.at[1]).start(),
-        shifted(1, 0, c.at[24:32, :], in_by.at[0], sb.at[2], rb.at[2]).start(),
-        shifted(1, 1, c.at[32:40, :], in_by.at[1], sb.at[3], rb.at[3]).start(),
+        shifted(1, 0, out_by.at[0], in_by.at[0], sb.at[2], rb.at[2]).start(),
+        shifted(1, 1, out_by.at[1], in_by.at[1], sb.at[3], rb.at[3]).start(),
     ] + z_ways
 
     for s in range(16):
@@ -317,6 +324,8 @@
     small = small + jnp.where(pz > 0, pltpu.roll(c[40:48, :], 1, 1), 0.0)
     small = small + jnp.where(pz < 31, pltpu.roll(c[56:64, :], N - 1, 1), 0.0)
     one = onehot[...].astype(BF16)
+    z_names = [onehot[pl.ds(0, 16, stride=32), :], onehot[pl.ds(31, 16, stride=32), :]]
+    z_names = jnp.concatenate(z_names * 2, 0).astype(BF16)
     r_hi, r_lo = halves(restrict[...])
     r_hi, r_lo = r_hi.astype(F32), r_lo.astype(F32)
     r_stack = jnp.concatenate([r_hi, r_hi, r_lo], 0).astype(BF16)
@@ -325,14 +334,18 @@
         copy.wait_recv()
     zeros_mid = jnp.zeros((8, 256), F32)
     small = small + jnp.concatenate([in_bx[0], zeros_mid, in_bx[1]], 1)
-    small = small + jnp.where(py == 0, pltpu.roll(in_by[0], N - 96, 1), 0.0)
-    small = small + jnp.where(py == 3, pltpu.roll(in_by[1], 96, 1), 0.0)
-    z_low, z_high = pltpu.roll(in_bz[0], N - 31, 1), pltpu.roll(in_bz[1], 31, 1)
-    small = small + jnp.where(pz == 0, z_low[0:8] + z_low[8:16] * c[48:56, :], 0.0)
-    small = small + jnp.where(pz == 31, z_high[8:16] + z_high[0:8] * c[48:56, :], 0.0)
+    below = [jnp.where(quarter == 0, pltpu.roll(in_by[0], turn, 1), 0.0) for turn in (0, 96, 64, 32)]
+    above = [jnp.where(quarter == 3, pltpu.roll(in_by[1], turn, 1), 0.0) for turn in (96, 64, 32, 0)]
+    small = small + jnp.concatenate([a + b for a, b in zip(below, above)], 1)
+    z_low = in_bz[0] + pltpu.roll(in_bz[0], 120, 1) * more[48:64]
+    z_high = in_bz[1] + pltpu.roll(in_bz[1], 8, 1) * more[32:48]
+    z_add = jnp.concatenate([jnp.where(lane16 // 8 == 5, z_low, 0.0), jnp.where(lane16 // 8 == 7, z_high, 0.0)], 0)
+    n_hi, n_lo = halves(z_add)
+    z_add = jnp.concatenate([n_hi.astype(F32), n_lo.astype(F32)], 0).astype(BF16)
+    z_add = lax.dot_general(z_add, z_names, TN, preferred_element_type=F32)
     m_hi, m_lo = halves(small)
     parts = dot1(jnp.concatenate([m_hi.astype(F32), m_lo.astype(F32)], 0).astype(BF16), one)
-    coarse_rhs = parts[0:8] + parts[8:16]
+    coarse_rhs = parts[0:8] + parts[8:16] + (z_add[40:48] + z_add[56:64])
     zone = coarse_rhs * per
     zone_out[...] = zone
 
@@ -402,10 +415,11 @@
             pltpu.VMEM((2, 16, 128), F32),
             pltpu.VMEM((2, 16, 128), F32),
             pltpu.VMEM((FACE, N), F32),
-            pltpu.VMEM((24, N), F32),
             pltpu.VMEM((2, 8, 128), F32),
-            pltpu.VMEM((2, 8, N), F32),
-            pltpu.VMEM((2, 16, N), F32),
+            pltpu.VMEM((2, 16, 128), F32),
+            pltpu.VMEM((2, 8, 128), F32),
+            pltpu.VMEM((2, 8, 128), F32),
+            pltpu.VMEM((2, 16, 128), F32),
             pltpu.VMEM((8, 128), F32),
             pltpu.VMEM((others, 8, 128), F32),
             dma((10,)),

time: 30 us -> 29.8 us (level)
  no operation moved by 1% of the time
where the time goes in v5:
time: 29.8 us; the launch traced here: 29.7 us
  Pallas kernels  28.7 us (96%)
  local copies, waits for them, and re-layouts  0.97 us (3%)
    pallas_call x1, Pallas kernels, shards(): pl.pallas_call(functools.partial(kernel, sizes), out_shape=pltpu.VMEM((N,...  28.7 us
    unnamed x1, local copies, waits for them, and re-layouts  0.97 us

profile of v5, /device:TPU:1, one launch (start us, length us, event | category | flops | bytes accessed | tf_op | source)
XLA Modules:
  0.0 29.7 jit_solution(618121455601092781)
XLA Ops:
  0.0 28.7 %cycle.1 = f32[512,512]{1,0:T(8,128)S(1)} custom-call(f32[512,512]{1,0:T(8,128)} %bitcast.4, f32[4,4,32]{2,1,0:T(4,128)} %coef_hbm.1, f32[512,512]{1,0:T(8,128)} %mass_hbm.1, f32[512,512]{1,0:T(8,128)} %smoother_hbm.1, f32[384,512]{1,0:T(8,128)} %lift_hbm.1, f32[8,512]{1,0:T(8,128)} %bitcast.5, f32[8,8]{1,0:T(8,128)} %cbm_hbm.1, s32[4,4,32]{2,1,0:T(4,128)} %label_hbm.1), custom_call_target="tpu_custom_call" | custom-call | tf_op jit(solution)/shard_map/cycle/pallas_call | solution.py:388
  28.7 1.0 %copy.10 = f32[4,4,32,512]{3,2,1,0:T(8,128)} copy(f32[4,4,32,512]{3,2,1,0:T(8,128)S(1)} %bitcast.3) | data formatting | bytes 2097152

commit v6 on v5

--- a/solution.py
+++ b/solution.py
@@ -38,12 +38,32 @@
     sizes, rhs_hbm, coef_hbm, mass_hbm, smoother_hbm, lift_hbm, restrict_hbm, cbm_hbm, label_hbm,
     out_ref,
     rhs, mass, smoother, lift, restrict, cbm, coef, label,
-    dcol, onehot, pick, u, first, tr, faces, v, lsg, wide, rows_z,
+    dcol, onehot, pick, u, first, tr, faces, v, lsg, wide, scatter, s_off, m_hi, m_lo,
     out_a, in_a, out_z, in_z, c, out_by, out_bz, in_bx, in_by, in_bz, zone_out, in_zone,
     load_sem, sa, ra, sb, rb, sz, rz,
 ):
     ngx, ngy, ngz = sizes
     places = [lax.axis_index(axis) for axis in ("gx", "gy", "gz")]
+
+    def along(dim, step):
+        size = sizes[dim]
+        return {("gx", "gy", "gz")[dim]: lax.rem(places[dim] + (step + size), size)}
+
+    beside = [(along(dim, 1), along(dim, -1)) for dim in range(3)]
+    there = [(places[dim] < sizes[dim] - 1, places[dim] > 0) for dim in range(3)]
+    line = [along(0, step) for step in range(1, ngx)]
+
+    barrier = pltpu.get_barrier_semaphore()
+    partners = ngx - 1
+    for dim in (2, 1):
+        for way in (0, 1):
+            partners = partners + jnp.where(there[dim][way], 1, 0)
+
+            @pl.when(there[dim][way])
+            def _():
+                pl.semaphore_signal(barrier, inc=1, device_id=beside[dim][way], device_id_type=MESH)
+    for device in line:
+        pl.semaphore_signal(barrier, inc=1, device_id=device, device_id_type=MESH)
 
     loads = [
         pltpu.make_async_copy(src, dst, load_sem.at[n])
@@ -65,26 +85,6 @@
     for copy in loads:
         copy.start()
 
-    def along(dim, step):
-        size = sizes[dim]
-        return {("gx", "gy", "gz")[dim]: lax.rem(places[dim] + (step + size), size)}
-
-    beside = [(along(dim, 1), along(dim, -1)) for dim in range(3)]
-    there = [(places[dim] < sizes[dim] - 1, places[dim] > 0) for dim in range(3)]
-    line = [along(0, step) for step in range(1, ngx)]
-
-    barrier = pltpu.get_barrier_semaphore()
-    for device in line:
-        pl.semaphore_signal(barrier, inc=1, device_id=device, device_id_type=MESH)
-    partners = ngx - 1
-    for dim in (1, 2):
-        for way in (0, 1):
-            partners = partners + jnp.where(there[dim][way], 1, 0)
-
-            @pl.when(there[dim][way])
-            def _():
-                pl.semaphore_signal(barrier, inc=1, device_id=beside[dim][way], device_id_type=MESH)
-
     class Message:
         def __init__(self, src, dst, send_sem, recv_sem, device, goes, comes):
             self.copy = pltpu.make_async_remote_copy(
@@ -159,39 +159,31 @@
     u[...] = dot3(rhs[...], smoother[...])
     first[...] = u[...] * d4(dcol[...])
 
-    for s in range(16):
-        rows_z[s : s + 1, :] = first[32 * s + 31 : 32 * s + 32, :]
-        rows_z[16 + s : 17 + s, :] = first[32 * s : 32 * s + 1, :]
-    ends = rows_z[...]
-    e_hi, e_lo = halves(ends)
-    ends = dot1(e_hi, pick[:, 128:256]) + dot1(e_lo, pick[:, 128:256])
-    out_z[0] = ends[0:16]
-    out_z[1] = ends[16:32]
-    pl.semaphore_wait(barrier, partners)
-    z_traces = [
-        shifted(2, way, out_z.at[way], in_z.at[way], sa.at[4 + way], ra.at[4 + way]).start()
-        for way in (0, 1)
-    ]
-
     low = iota((FACE, 128), 1) < FACE
     swap = lambda a: pltpu.roll(a, FACE, 1)
     top, bottom = first[384:512, 384:512], first[0:128, 0:128]
     out_a[0] = jnp.where(low, swap(top[0:64]), top[64:128])
     out_a[1] = jnp.where(low, bottom[0:64], swap(bottom[64:128]))
-    a_copies = [
-        shifted(0, way, out_a.at[way], in_a.at[way], sa.at[way], ra.at[way]).start() for way in (0, 1)
-    ]
-
     f_hi, f_lo = halves(first[...])
     tr[...] = dot1(f_hi, pick[...]) + dot1(f_lo, pick[...])
     ytop = [tr[128 * i + 96 : 128 * i + 128, 0:128] for i in range(4)]
     ybottom = [tr[128 * i : 128 * i + 32, 0:128] for i in range(4)]
     out_a[2] = jnp.where(low, jnp.concatenate(ytop[:2], 0), swap(jnp.concatenate(ytop[2:], 0)))
     out_a[3] = jnp.where(low, swap(jnp.concatenate(ybottom[:2], 0)), jnp.concatenate(ybottom[2:], 0))
-    a_copies += [
-        shifted(1, way, out_a.at[2 + way], in_a.at[2 + way], sa.at[2 + way], ra.at[2 + way]).start()
+    for i in range(16):
+        out_z[0, i : i + 1, :] = tr[32 * i + 31 : 32 * i + 32, 128:256]
+        out_z[1, i : i + 1, :] = tr[32 * i : 32 * i + 1, 128:256]
+    pl.semaphore_wait(barrier, partners)
+    z_traces = [
+        shifted(2, way, out_z.at[way], in_z.at[way], sa.at[4 + way], ra.at[4 + way]).start()
         for way in (0, 1)
     ]
+    a_copies = [
+        shifted(dim, way, out_a.at[2 * dim + way], in_a.at[2 * dim + way], sa.at[2 * dim + way], ra.at[2 * dim + way]).start()
+        for dim in (1, 0)
+        for way in (0, 1)
+    ]
+
     for copy in loads[4:]:
         copy.wait()
 
@@ -214,17 +206,42 @@
     r_wide = many.T
     r_table = table(r_wide)
     lift_r = jnp.where(kind == jnp.where(block < 5, block + 1, 7), project(lift[...], r_table), 0.0)
-    g = jnp.where(lane_n % 64 < 8, -project(mass[...], r_table), 0.0)
-    l_hi, l_lo = halves(lift_r[128:384])
-    g = g + (dot1(pick[...], l_hi) + dot1(pick[...], l_lo))
-    g = g + jnp.concatenate([lift_r[0:64], jnp.zeros((384, 128), F32), lift_r[64:128]], 0)
-    sg = project(smoother[...], table(g))
+    unit = jnp.where(iota((128, 128), 0) == iota((128, 128), 1), 1.0, 0.0)
+    m_hi[...], m_lo[...] = halves(mass[...])
+    for i in range(4):
+        part = slice(128 * i, 128 * i + 128)
+        m_hi[part, part], m_lo[part, part] = halves(mass[part, part] - unit)
+
+    def mass_rest(columns):
+        t = dot1(m_hi[...], columns[0]) + dot1(m_lo[...], columns[1])
+        return t + swap(t)
+
+    scatter[...] = jnp.where(lane_n % 64 < 8, -(r_wide + mass_rest(r_table)), 0.0)
+    scatter[0:64, :] = scatter[0:64, :] + lift_r[0:64]
+    scatter[448:512, :] = scatter[448:512, :] + lift_r[64:128]
+    for i in range(8):
+        for j, at in ((7, 128), (0, 192)):
+            rows = slice(64 * i + 8 * j, 64 * i + 8 * j + 8)
+            scatter[rows, :] = scatter[rows, :] + lift_r[at + 8 * i : at + 8 * i + 8]
+    for k, at in ((7, 256), (0, 320)):
+        rows = pl.ds(k, FACE, stride=8)
+        scatter[rows, :] = scatter[rows, :] + lift_r[at : at + FACE]
+    g = scatter[...]
+
+    s_off[...] = smoother[...].astype(BF16)
+    for i in range(4):
+        part = slice(128 * i, 128 * i + 128)
+        s_off[part, part] = (smoother[part, part] - unit).astype(BF16)
+    t = dot1(s_off[...], table(g)[0])
+    s_rest = t + swap(t)
+    sg = g + s_rest
     sg_table = table(sg)
     lsg[...] = project(lift[...], sg_table)
     l_table = table(lsg[...])
-    msg = project(mass[...], sg_table)
+    small_g = -(s_rest + mass_rest(sg_table))
     own = jnp.where(lane_n % 64 < 8, r_wide, 0.0)
-    wide[...] = project(rhs[...], table(sg + own)) + project(u[...], table(g - msg))
+    t = dot1(u[...].astype(BF16), table(small_g)[0])
+    wide[...] = project(rhs[...], table(sg + own)) + (t + swap(t))
     weight = 1.0 + jnp.sum(onehot[...], 0, keepdims=True)
     weight = jnp.broadcast_to(weight, (8, 128))
     per = 1.0 / weight
@@ -311,7 +328,8 @@
         faces[at : at + 1, 256:384] = jnp.where(lane[0:1] < FACE, in_z[0, s : s + 1, :], faces[at : at + 1, 256:384])
         at = 32 * s + 31
         faces[at : at + 1, 256:384] = jnp.where(lane[0:1] < FACE, faces[at : at + 1, 256:384], in_z[1, s : s + 1, :])
-    v[...] = rhs[...] - dot3(u[...], mass[...])
+    u_hi, u_lo = halves(u[...])
+    v[...] = rhs[...] - (u[...] + (dot1(u_hi, m_hi[...]) + dot1(u_lo, m_hi[...]) + dot1(u_hi, m_lo[...])))
 
     small = c[0:8, :]
     none8 = jnp.zeros((8, 128), F32)
@@ -343,8 +361,8 @@
     n_hi, n_lo = halves(z_add)
     z_add = jnp.concatenate([n_hi.astype(F32), n_lo.astype(F32)], 0).astype(BF16)
     z_add = lax.dot_general(z_add, z_names, TN, preferred_element_type=F32)
-    m_hi, m_lo = halves(small)
-    parts = dot1(jnp.concatenate([m_hi.astype(F32), m_lo.astype(F32)], 0).astype(BF16), one)
+    q_hi, q_lo = halves(small)
+    parts = dot1(jnp.concatenate([q_hi.astype(F32), q_lo.astype(F32)], 0).astype(BF16), one)
     coarse_rhs = parts[0:8] + parts[8:16] + (z_add[40:48] + z_add[56:64])
     zone = coarse_rhs * per
     zone_out[...] = zone
@@ -409,7 +427,10 @@
             pltpu.VMEM((N, N), F32),
             pltpu.VMEM((384, 128), F32),
             pltpu.VMEM((N, 128), F32),
-            pltpu.VMEM((32, N), F32),
+            pltpu.VMEM((N, 128), F32),
+            pltpu.VMEM((N, N), BF16),
+            pltpu.VMEM((N, N), BF16),
+            pltpu.VMEM((N, N), BF16),
             pltpu.VMEM((4, FACE, 128), F32),
             pltpu.VMEM((4, FACE, 128), F32),
             pltpu.VMEM((2, 16, 128), F32),

time: 29.8 us -> 29 us (0.973)
  Pallas kernels: 28.7 us -> 27.9 us
    pallas_call x1, Pallas kernels: 28.7 us -> 27.9 us  [shards(): pl.pallas_call(functools.partial(kernel, sizes), out_shape=pltpu.VMEM((N,...]
where the time goes in v6:
time: 29 us; the launch traced here: 28.9 us
  Pallas kernels  27.9 us (96%)
  local copies, waits for them, and re-layouts  0.97 us (3%)
    pallas_call x1, Pallas kernels, shards(): pl.pallas_call(functools.partial(kernel, sizes), out_shape=pltpu.VMEM((N,...  27.9 us
    unnamed x1, local copies, waits for them, and re-layouts  0.97 us

profile of v6, /device:TPU:1, one launch (start us, length us, event | category | flops | bytes accessed | tf_op | source)
XLA Modules:
  0.0 28.9 jit_solution(353281013098857309)
XLA Ops:
  0.0 27.9 %cycle.1 = f32[512,512]{1,0:T(8,128)S(1)} custom-call(f32[512,512]{1,0:T(8,128)} %bitcast.4, f32[4,4,32]{2,1,0:T(4,128)} %coef_hbm.1, f32[512,512]{1,0:T(8,128)} %mass_hbm.1, f32[512,512]{1,0:T(8,128)} %smoother_hbm.1, f32[384,512]{1,0:T(8,128)} %lift_hbm.1, f32[8,512]{1,0:T(8,128)} %bitcast.5, f32[8,8]{1,0:T(8,128)} %cbm_hbm.1, s32[4,4,32]{2,1,0:T(4,128)} %label_hbm.1), custom_call_target="tpu_custom_call" | custom-call | tf_op jit(solution)/shard_map/cycle/pallas_call | solution.py:406
  27.9 1.0 %copy.10 = f32[4,4,32,512]{3,2,1,0:T(8,128)} copy(f32[4,4,32,512]{3,2,1,0:T(8,128)S(1)} %bitcast.3) | data formatting | bytes 2097152

commit v7 on v6

--- a/solution.py
+++ b/solution.py
@@ -263,8 +263,61 @@
         above = jnp.where(row == 31, 0.0, pltpu.roll(own, 31, 0))
         faces[rows, 256:384] = jnp.where(low32, below, above)
 
+    wide[...] = wide[...] + project(faces[...], l_table)
+    low16 = iota((16, 128), 1) < FACE
+    ends = jnp.concatenate([jnp.where(low16, out_z[0], 0.0), jnp.where(low16, 0.0, out_z[1])], 0)
+    back = dot3(ends, lsg[256:384, :])
+    none64 = jnp.zeros((FACE, 128), BF16)
+
+    def twice(a):
+        return jnp.concatenate([jnp.concatenate([a, none64], 1), jnp.concatenate([none64, a], 1)], 0)
+
+    packed_table = [[twice(part[at : at + FACE]) for part in l_table] for at in (64, 0, 128, 192)]
+
     for copy in a_copies:
         copy.wait_recv()
+    for n in range(4):
+        hi, lo = halves(in_a[n])
+        t = dot1(hi, packed_table[n][0]) + dot1(lo, packed_table[n][1])
+        parts = [t[:, 0:128] + swap(t[:, 0:128]), t[:, 128:256] + swap(t[:, 128:256])]
+        for i in range(4):
+            part = parts[i // 2][32 * (i % 2) : 32 * (i % 2) + 32]
+            at = (32 * i, 384 + 32 * i, 128 * i, 128 * i + 96)[n]
+            wide[at : at + 32, :] = wide[at : at + 32, :] + part
+    lane16 = iota((16, 128), 1)
+    for way, at in ((0, 31), (1, 0)):
+        d_ends = dcol[pl.ds(at, 16, stride=32), :]
+        out_bz[way] = jnp.where(lane16 // 8 == 6, d_ends, d_ends * wide[pl.ds(at, 16, stride=32), :])
+    z_ways = [
+        shifted(2, way, out_bz.at[way], in_bz.at[way], sb.at[4 + way], rb.at[4 + way]).start() for way in (0, 1)
+    ]
+
+    for copy in z_traces:
+        copy.wait_recv()
+    ends = jnp.concatenate([jnp.where(low16, in_z[0], 0.0), jnp.where(low16, 0.0, in_z[1])], 0)
+    more = dot3(ends, lsg[256:384, :])
+    wide[pl.ds(0, 16, stride=32), :] = wide[pl.ds(0, 16, stride=32), :] + more[0:16]
+    wide[pl.ds(31, 16, stride=32), :] = wide[pl.ds(31, 16, stride=32), :] + more[16:32]
+    w = wide[...].T
+    c[...] = jnp.concatenate([w[0:8], w[8:64] * d_row], 0)
+    quarter = iota((8, 128), 1) // 32
+
+    def gather_y(tiles, turns):
+        packed = jnp.zeros((8, 128), F32)
+        for i in range(4):
+            packed = jnp.where(quarter == i, pltpu.roll(tiles[i], turns[i], 1), packed)
+        return packed
+
+    out_by[0] = gather_y([c[24:32, 128 * i : 128 * i + 128] for i in range(4)], [32, 64, 96, 0])
+    out_by[1] = gather_y([c[32:40, 128 * i : 128 * i + 128] for i in range(4)], [0, 32, 64, 96])
+
+    b_copies = [
+        shifted(0, 0, c.at[16:24, 384:512], in_bx.at[0], sb.at[0], rb.at[0]).start(),
+        shifted(0, 1, c.at[8:16, 0:128], in_bx.at[1], sb.at[1], rb.at[1]).start(),
+        shifted(1, 0, out_by.at[0], in_by.at[0], sb.at[2], rb.at[2]).start(),
+        shifted(1, 1, out_by.at[1], in_by.at[1], sb.at[3], rb.at[3]).start(),
+    ] + z_ways
+
     faces[0:64, 0:128] = jnp.where(low, faces[0:64, 0:128], swap(in_a[0]))
     faces[64:128, 0:128] = jnp.where(low, faces[64:128, 0:128], in_a[0])
     faces[384:448, 0:128] = jnp.where(low, in_a[1], faces[384:448, 0:128])
@@ -278,50 +331,6 @@
         faces[j : j + 32, 128:256] = jnp.where(low32, below, faces[j : j + 32, 128:256])
         j = 128 * i + 96
         faces[j : j + 32, 128:256] = jnp.where(low32, faces[j : j + 32, 128:256], above)
-
-    wide[...] = wide[...] + project(faces[...], l_table)
-    lane16 = iota((16, 128), 1)
-    for way, at in ((0, 31), (1, 0)):
-        d_ends = dcol[pl.ds(at, 16, stride=32), :]
-        out_bz[way] = jnp.where(lane16 // 8 == 6, d_ends, d_ends * wide[pl.ds(at, 16, stride=32), :])
-    z_ways = [
-        shifted(2, way, out_bz.at[way], in_bz.at[way], sb.at[4 + way], rb.at[4 + way]).start() for way in (0, 1)
-    ]
-
-    for copy in z_traces:
-        copy.wait_recv()
-    low16 = iota((16, 128), 1) < FACE
-    ends = jnp.concatenate(
-        [
-            jnp.where(low16, in_z[0], 0.0),
-            jnp.where(low16, 0.0, in_z[1]),
-            jnp.where(low16, out_z[0], 0.0),
-            jnp.where(low16, 0.0, out_z[1]),
-        ],
-        0,
-    )
-    more = dot3(ends, lsg[256:384, :])
-    wide[pl.ds(0, 16, stride=32), :] = wide[pl.ds(0, 16, stride=32), :] + more[0:16]
-    wide[pl.ds(31, 16, stride=32), :] = wide[pl.ds(31, 16, stride=32), :] + more[16:32]
-    w = wide[...].T
-    c[...] = jnp.concatenate([w[0:8], w[8:64] * d_row], 0)
-    quarter = iota((8, 128), 1) // 32
-
-    def gather_y(tiles, turns):
-        packed = jnp.zeros((8, 128), F32)
-        for i in range(4):
-            packed = jnp.where(quarter == i, pltpu.roll(tiles[i], turns[i], 1), packed)
-        return packed
-
-    out_by[0] = gather_y([c[24:32, 128 * i : 128 * i + 128] for i in range(4)], [32, 64, 96, 0])
-    out_by[1] = gather_y([c[32:40, 128 * i : 128 * i + 128] for i in range(4)], [0, 32, 64, 96])
-
-    b_copies = [
-        shifted(0, 0, c.at[16:24, 384:512], in_bx.at[0], sb.at[0], rb.at[0]).start(),
-        shifted(0, 1, c.at[8:16, 0:128], in_bx.at[1], sb.at[1], rb.at[1]).start(),
-        shifted(1, 0, out_by.at[0], in_by.at[0], sb.at[2], rb.at[2]).start(),
-        shifted(1, 1, out_by.at[1], in_by.at[1], sb.at[3], rb.at[3]).start(),
-    ] + z_ways
 
     for s in range(16):
         at = 32 * s
@@ -355,8 +364,8 @@
     below = [jnp.where(quarter == 0, pltpu.roll(in_by[0], turn, 1), 0.0) for turn in (0, 96, 64, 32)]
     above = [jnp.where(quarter == 3, pltpu.roll(in_by[1], turn, 1), 0.0) for turn in (96, 64, 32, 0)]
     small = small + jnp.concatenate([a + b for a, b in zip(below, above)], 1)
-    z_low = in_bz[0] + pltpu.roll(in_bz[0], 120, 1) * more[48:64]
-    z_high = in_bz[1] + pltpu.roll(in_bz[1], 8, 1) * more[32:48]
+    z_low = in_bz[0] + pltpu.roll(in_bz[0], 120, 1) * back[16:32]
+    z_high = in_bz[1] + pltpu.roll(in_bz[1], 8, 1) * back[0:16]
     z_add = jnp.concatenate([jnp.where(lane16 // 8 == 5, z_low, 0.0), jnp.where(lane16 // 8 == 7, z_high, 0.0)], 0)
     n_hi, n_lo = halves(z_add)
     z_add = jnp.concatenate([n_hi.astype(F32), n_lo.astype(F32)], 0).astype(BF16)

time: 29 us -> 28.7 us (0.990)
  Pallas kernels: 27.9 us -> 27.5 us
    pallas_call x1, Pallas kernels: 27.9 us -> 27.5 us  [shards(): pl.pallas_call(functools.partial(kernel, sizes), out_shape=pltpu.VMEM((N,...]
where the time goes in v7:
time: 28.7 us; the launch traced here: 28.5 us
  Pallas kernels  27.5 us (96%)
  local copies, waits for them, and re-layouts  0.97 us (3%)
    pallas_call x1, Pallas kernels, shards(): pl.pallas_call(functools.partial(kernel, sizes), out_shape=pltpu.VMEM((N,...  27.5 us
    unnamed x1, local copies, waits for them, and re-layouts  0.97 us

profile of v7, /device:TPU:1, one launch (start us, length us, event | category | flops | bytes accessed | tf_op | source)
XLA Modules:
  0.0 28.5 jit_solution(10945397545059578019)
XLA Ops:
  0.0 27.5 %cycle.1 = f32[512,512]{1,0:T(8,128)S(1)} custom-call(f32[512,512]{1,0:T(8,128)} %bitcast.4, f32[4,4,32]{2,1,0:T(4,128)} %coef_hbm.1, f32[512,512]{1,0:T(8,128)} %mass_hbm.1, f32[512,512]{1,0:T(8,128)} %smoother_hbm.1, f32[384,512]{1,0:T(8,128)} %lift_hbm.1, f32[8,512]{1,0:T(8,128)} %bitcast.5, f32[8,8]{1,0:T(8,128)} %cbm_hbm.1, s32[4,4,32]{2,1,0:T(4,128)} %label_hbm.1), custom_call_target="tpu_custom_call" | custom-call | tf_op jit(solution)/shard_map/cycle/pallas_call | solution.py:415
  27.5 1.0 %copy.10 = f32[4,4,32,512]{3,2,1,0:T(8,128)} copy(f32[4,4,32,512]{3,2,1,0:T(8,128)S(1)} %bitcast.3) | data formatting | bytes 2097152
